TPU v7x, 32 devices: a whole 2x2x4 slice. The times are simulated.
32 devices in a mesh: rep: 4 (over y, core), shard: 8 (over z, x).
Axes of the slice: x: 2, y: 2, z: 4, core: 2. Of those that a mesh axis runs over, the one named last changes fastest.
Arguments:
- grad_part: bfloat16 [4, 4096, 512], P('rep', 'shard'), may hold values from -10.5 to 10.5
- seg_slot: int32 [8, 512], replicated, may hold values from 0 to 4095, as said below
- owner: int32 [8], replicated, may hold values from 0 to 7, as said below
- left_code: bfloat16 [16, 512, 512], P('shard'), may hold values from -127 to 127, as said below
- left_scale: float32 [16, 512], P('shard'), may hold values from 0.0023622 to 0.023622
- right_code: bfloat16 [16, 512, 512], P('shard'), may hold values from -127 to 127, as said below
- right_scale: float32 [16, 512], P('shard'), may hold values from 0.0023622 to 0.023622
Outputs:
- update: bfloat16 [4096, 512], P('shard')
Inputs may be any that keep to these rules, and one draw needn't show every extreme that they name: `seg_slot`: every flat segment index appears once; row i of block b lies in shard (i + c) mod 8, where c, drawn for each block, is the shard of its row 0, and shard k holds the segment indices k * 512 to (k + 1) * 512 - 1. `owner`: no shard index owns more than 2 blocks, and one owns exactly 2. `left_code`: whole numbers; each row's largest code has magnitude 127. `right_code`: whole numbers; each column's largest code has magnitude 127.
All inputs are finite; a program needn't handle non-finite values.
Results may differ from a plain program's by a relative error of at most 0.025.
Values may be sent and summed in bfloat16 or wider, within the bound.
A program may use at most 64 MiB of HBM per device.

v0:
```python
import jax
import jax.numpy as jnp
from jax import lax
from jax.sharding import PartitionSpec as P

EPSILON = 1e-06


def owner_tables(owner, slot_count, shards):
    block_ids = jnp.arange(owner.shape[0], dtype=jnp.int32)
    same_owner = owner[None, :] == owner[:, None]
    earlier = block_ids[None, :] < block_ids[:, None]
    slot_rank = jnp.sum((same_owner & earlier).astype(jnp.int32), axis=1)
    slot_index = owner * slot_count + slot_rank
    wanted = jnp.arange(shards * slot_count, dtype=jnp.int32)
    matches = slot_index[:, None] == wanted[None, :]
    block_of = jnp.sum(jnp.where(matches, block_ids[:, None], 0), axis=0)
    filled = jnp.any(matches, axis=0)
    return (block_of.reshape(shards, slot_count), filled.reshape(shards, slot_count))


def on_device(grad_part, seg_slot, owner, left_code, left_scale, right_code, right_scale):
    shards = lax.axis_size("shard")
    own_index = lax.axis_index("shard")
    seg_local = grad_part.shape[1]
    block_width = grad_part.shape[2]
    slot_count = left_code.shape[0]
    rows_shard = block_width // shards
    block_of, filled = owner_tables(owner, slot_count, shards)
    first_shard = seg_slot[:, 0] // seg_local
    block_shift = jnp.where(filled, first_shard[block_of], 0)
    dest_shard = jnp.arange(shards, dtype=jnp.int32)[:, None, None]
    row_step = jnp.arange(rows_shard, dtype=jnp.int32)[None, None, :]
    row_sent = shards * row_step + (own_index - block_shift[:, :, None]) % shards
    in_use = jnp.broadcast_to(filled[:, :, None], row_sent.shape)
    position = jnp.where(
        in_use, seg_slot[block_of[:, :, None], row_sent] - own_index * seg_local, 0
    )
    summed = lax.psum(grad_part[0].astype(jnp.float32).astype(jnp.bfloat16), "rep")
    outgoing = jnp.where(in_use[..., None], summed[position], jnp.zeros((), jnp.bfloat16))
    arrived = lax.all_to_all(outgoing, "shard", split_axis=0, concat_axis=0, tiled=True)
    mine_shift = block_shift[own_index]
    full_rows = jnp.arange(block_width, dtype=jnp.int32)
    source = (full_rows[None, :] % shards + mine_shift[:, None]) % shards
    slot_ids = jnp.arange(slot_count, dtype=jnp.int32)[:, None]
    block_grad = arrived[source, slot_ids, full_rows[None, :] // shards]
    middle = jnp.einsum("kij,kjl->kil", block_grad, right_code, preferred_element_type=jnp.float32)
    middle = (middle * right_scale[:, None, :]).astype(jnp.bfloat16)
    precond = jnp.einsum("kij,kjl->kil", left_code, middle, preferred_element_type=jnp.float32)
    precond = precond * left_scale[:, :, None]
    grad_wide = block_grad.astype(jnp.float32)
    grad_power = jnp.mean(grad_wide * grad_wide, axis=(1, 2))
    update_power = jnp.mean(precond * precond, axis=(1, 2))
    graft_ratio = jnp.sqrt((grad_power + EPSILON) / (update_power + EPSILON))
    update_block = (precond * graft_ratio[:, None, None]).astype(jnp.bfloat16)
    dest_rows = shards * row_step + (dest_shard - mine_shift[None, :, None]) % shards
    backward = update_block[jnp.arange(slot_count, dtype=jnp.int32)[None, :, None], dest_rows]
    target = jnp.where(in_use, position, seg_local)
    returned = lax.all_to_all(backward, "shard", split_axis=0, concat_axis=0, tiled=True)
    update = jnp.zeros((seg_local, block_width), jnp.bfloat16)
    update = update.at[target.reshape(-1)].set(returned.reshape(-1, block_width), mode="drop")
    return update


def solution(mesh):
    in_specs = (
        P("rep", "shard", None),
        P(),
        P(),
        P("shard", None, None),
        P("shard", None),
        P("shard", None, None),
        P("shard", None),
    )
    out_specs = P("shard", None)
    return jax.shard_map(
        on_device, mesh=mesh, in_specs=in_specs, out_specs=out_specs, check_vma=False
    )
```

profile of v0, /device:TPU:0, one launch (start us, length us, event | category | flops | bytes accessed | tf_op | source)
XLA Modules:
  0.0 152.1 jit_solution(3324372614133322788)
XLA Ops:
  6.5 0.7 all-reduce.2.cloned.1.call-update
  7.3 0.9 convert_reduce_fusion
  8.2 0.7 multiply_add_fusion
  8.8 0.1 select_reduce_fusion
  8.9 0.1 fusion.23
  9.2 0.8 slice_reduce_fusion
  10.2 0.7 gather_fusion
  11.0 0.1 fusion.10
  11.2 6.8 %gather_fusion.1 = s32[1024]{0:T(1024)S(1)} fusion(s32[8,512]{1,0:T(8,128)S(1)} %copy-done.1, s32[1024]{0:T(1024)S(1)} %reshape.382), kind=kCustom, calls=%fused_computation.1 | custom fusion | bytes 16384 | tf_op jit(solution)/shard_map/gather | solution.py:37
  18.2 27.4 %all-reduce.2.cloned.1.call-done = bf16[512,512]{1,0:T(8,128)(2,1)} async-done(((bf16[512,512]{1,0:T(8,128)(2,1)}), bf16[512,512]{1,0:T(8,128)(2,1)}) %all-reduce.2.cloned.1.call-update) | async-done | bytes 524304 | tf_op jit(solution)/shard_map/psum | solution.py:39
  45.6 5.1 %gather_fusion.2 = bf16[1024,512]{1,0:T(8,128)(2,1)S(1)} fusion(bf16[512,512]{1,0:T(8,128)(2,1)} %all-reduce.2.cloned.1.call-done, s32[1024]{0:T(1024)S(1)} %broadcast_clamp_fusion), kind=kCustom, calls=%fused_computation.2 | custom fusion | bytes 2101248 | tf_op jit(solution)/shard_map/gather | solution.py:40
  50.7 1.1 broadcast_select_fusion
  51.9 5.5 %all-to-all-start = ((bf16[8,2,64,512]{3,2,1,0:T(8,128)(2,1)}), bf16[8,2,64,512]{3,2,1,0:T(8,128)(2,1)S(1)}, u32[]{:S(2)}, u32[]{:S(2)}) async-start(bf16[8,2,64,512]{3,2,1,0:T(8,128)(2,1)} %broadcast_select_fusion), calls=%async_computation | async-start | bytes 2097152 | tf_op jit(solution)/shard_map/all_to_all | solution.py:41
  57.6 24.9 %all-to-all-done = bf16[8,2,64,512]{3,2,1,0:T(8,128)(2,1)S(1)} async-done(((bf16[8,2,64,512]{3,2,1,0:T(8,128)(2,1)}), bf16[8,2,64,512]{3,2,1,0:T(8,128)(2,1)S(1)}, u32[]{:S(2)}, u32[]{:S(2)}) %all-to-all-start) | async-done | bytes 1048608 | tf_op jit(solution)/shard_map/all_to_all | solution.py:41
  82.4 8.5 %gather_fusion.3 = bf16[1024,512]{1,0:T(8,128)(2,1)S(1)} fusion(bf16[8,2,64,512]{3,2,1,0:T(8,128)(2,1)S(1)} %all-to-all-done, s32[1024]{0:T(1024)S(1)} %bitcast.27), kind=kCustom, calls=%fused_computation.3 | custom fusion | bytes 2109440 | tf_op jit(solution)/shard_map/gather | solution.py:46
  91.0 0.4 multiply_reduce_fusion.1
  91.4 3.8 %multiply_reduce_fusion = (f32[2]{0:T(128)S(1)}, f32[2,512,512]{2,1,0:T(8,128)}) fusion(f32[2,512]{1,0:T(2,128)S(1)} %copy-done.2, bf16[2,512,512]{2,1,0:T(8,128)(2,1)S(1)} %copy-done, bf16[2,512,512]{2,1,0:T(8,128)(2,1)S(1)} %bitcast.29, bf16[2,512,512]{2,1,0:T(8,128)(2,1)} %param.12, f32[2,512]{1,0:T(2,128)S(1)} %copy-done.3), kind=kOutput, calls=%fused_computation.7 | convolution fusion | flops 1076363264 | bytes 5251080 | tf_op jit(solution)/shard_map/kij,kjl->kil/dot_general | solution.py:49
  95.2 2.1 %fusion.1 = bf16[2,512,512]{1,2,0:T(8,128)(2,1)S(1)} fusion(f32[2,512,512]{2,1,0:T(8,128)} %get-tuple-element.10, f32[2]{0:T(128)S(1)} %fusion.33, f32[2,512]{1,0:T(2,128)S(1)} %copy-done.2), kind=kLoop, calls=%fused_computation.11 | loop fusion | flops 1572864 | bytes 3149832 | tf_op jit(solution)/shard_map/convert_element_type | solution.py:55
  97.3 0.5 copy.11
  97.8 12.3 %gather_fusion.4 = bf16[1024,512]{1,0:T(8,128)(2,1)} fusion(bf16[2,512,512]{2,1,0:T(8,128)(2,1)S(1)} %copy.11, s32[1024]{0:T(1024)S(1)} %reshape.402), kind=kCustom, calls=%fused_computation.4 | custom fusion | bytes 2105344 | tf_op jit(solution)/shard_map/gather | solution.py:57
  110.1 3.6 %all-to-all-start.1 = ((bf16[8,2,64,512]{3,2,1,0:T(8,128)(2,1)}), bf16[8,2,64,512]{3,2,1,0:T(8,128)(2,1)S(1)}, u32[]{:S(2)}, u32[]{:S(2)}) async-start(bf16[8,2,64,512]{3,2,1,0:T(8,128)(2,1)} %bitcast.7), calls=%async_computation.1 | async-start | bytes 2097152 | tf_op jit(solution)/shard_map/all_to_all | solution.py:59
  113.7 0.1 broadcast_in_dim.50
  113.9 25.6 %all-to-all-done.1 = bf16[8,2,64,512]{3,2,1,0:T(8,128)(2,1)S(1)} async-done(((bf16[8,2,64,512]{3,2,1,0:T(8,128)(2,1)}), bf16[8,2,64,512]{3,2,1,0:T(8,128)(2,1)S(1)}, u32[]{:S(2)}, u32[]{:S(2)}) %all-to-all-start.1) | async-done | bytes 1048608 | tf_op jit(solution)/shard_map/all_to_all | solution.py:59
  139.5 5.8 %scatter_custom_fusion = bf16[512,512]{1,0:T(8,128)(2,1)} fusion(s32[1024]{0:T(1024)S(1)} %bitcast.34, bf16[1024,512]{1,0:T(8,128)(2,1)S(1)} %bitcast.31, bf16[]{:T(256)} %constant.89.clone.1), kind=kCustom, calls=%fused_computation.14 | custom fusion | bytes 524290 | tf_op jit(solution)/shard_map/scatter | solution.py:61
  (34 shorter events, 1.1 us)
Async XLA Ops:
  6.5 84.8 %copy-start = (bf16[2,512,512]{2,1,0:T(8,128)(2,1)S(1)}, bf16[2,512,512]{2,1,0:T(8,128)(2,1)}, u32[]{:S(2)}) copy-start(bf16[2,512,512]{2,1,0:T(8,128)(2,1)} %param.10) | copy-start | bytes 3145732
  6.5 39.1 %all-reduce.2.cloned.1.call-start = ((), (), s32[]{:S(2)}) async-start(), calls=%async_computation.2 | async-start | bytes 1048576 | tf_op jit(solution)/shard_map/psum | solution.py:39
  10.2 1.0 copy-start.1
  51.9 30.6 %all-to-all-start = ((bf16[8,2,64,512]{3,2,1,0:T(8,128)(2,1)}), bf16[8,2,64,512]{3,2,1,0:T(8,128)(2,1)S(1)}, u32[]{:S(2)}, u32[]{:S(2)}) async-start(bf16[8,2,64,512]{3,2,1,0:T(8,128)(2,1)} %broadcast_select_fusion), calls=%async_computation | async-start | bytes 2097152 | tf_op jit(solution)/shard_map/all_to_all | solution.py:41
  82.4 8.9 %copy-start.2 = (f32[2,512]{1,0:T(2,128)S(1)}, f32[2,512]{1,0:T(2,128)}, u32[]{:S(2)}) copy-start(f32[2,512]{1,0:T(2,128)} %param.11) | copy-start | bytes 12292
  82.4 8.9 %copy-start.3 = (f32[2,512]{1,0:T(2,128)S(1)}, f32[2,512]{1,0:T(2,128)}, u32[]{:S(2)}) copy-start(f32[2,512]{1,0:T(2,128)} %param.13) | copy-start | bytes 12292
  110.1 29.4 %all-to-all-start.1 = ((bf16[8,2,64,512]{3,2,1,0:T(8,128)(2,1)}), bf16[8,2,64,512]{3,2,1,0:T(8,128)(2,1)S(1)}, u32[]{:S(2)}, u32[]{:S(2)}) async-start(bf16[8,2,64,512]{3,2,1,0:T(8,128)(2,1)} %bitcast.7), calls=%async_computation.1 | async-start | bytes 2097152 | tf_op jit(solution)/shard_map/all_to_all | solution.py:59
Sparse Core Ops, SparseCore 0:
  9.7 35.8 all-reduce.1
where the time goes:
time: 152 us
  waiting for transfers between devices  78.6 us (52%)
  local copies, waits for them, and re-layouts  41.3 us (27%)
  between operations  13.5 us (9%)
  starting transfers between devices  9.07 us (6%)
  other arithmetic  5.69 us (4%)
  matrix products  3.84 us (3%)
    psum x1, waiting for transfers between devices, on_device(): lax.psum(grad_part[0].astype(jnp.float32).astype(jnp.bfloat16), 'rep')  27.4 us
    all_to_all x1, waiting for transfers between devices, on_device(): lax.all_to_all(backward, 'shard', split_axis=0, concat_axis=0, tiled=True)  25.6 us
    all_to_all x1, waiting for transfers between devices, on_device(): lax.all_to_all(outgoing, 'shard', split_axis=0, concat_axis=0, tiled=True)  24.9 us
    gather x1, local copies, waits for them, and re-layouts, on_device(): update_block[jnp.arange(slot_count, dtype=jnp.int32)[None, :, None], dest...  12.3 us
    gather x1, local copies, waits for them, and re-layouts, on_device(): block_grad = arrived[source, slot_ids, full_rows[None, :] // shards]  8.52 us
    gather x1, local copies, waits for them, and re-layouts, on_device(): seg_slot[block_of[:, :, None], row_sent] - own_index * seg_local  6.76 us
    scatter x1, local copies, waits for them, and re-layouts, on_device(): update.at[target.reshape(-1)]  5.78 us
    all_to_all x1, starting transfers between devices, on_device(): lax.all_to_all(outgoing, 'shard', split_axis=0, concat_axis=0, tiled=True)  5.51 us
  transfers between devices with their start and end apart: 3, of which 3 were waited for; matrix products, arithmetic and copies ran while one was open for 7% of the time, Pallas kernels for 0%

commit v1 on v0

v1 whole, which is shorter than its diff:
```python
import functools

import jax
import jax.numpy as jnp
from jax import lax
from jax.experimental import pallas as pl
from jax.experimental.pallas import tpu as pltpu
from jax.sharding import PartitionSpec as P

EPSILON = 1e-06
MESH = pl.DeviceIdType.MESH
F32 = jnp.float32
BF16 = jnp.bfloat16
Y_OUT, Z_OUT, C_OUT, Z_BACK, Y_BACK, C_BACK, C_BACK_FAR, PAIR = range(8)


def log2(value):
    assert value & (value - 1) == 0
    return value.bit_length() - 1


def iota(shape, dim):
    return lax.broadcasted_iota(jnp.int32, shape, dim)


def one_hot(mask):
    return jnp.where(mask, 1.0, 0.0).astype(BF16)


def dot(a, b, contract=((1,), (0,))):
    return lax.dot_general(a, b, (contract, ((), ())), preferred_element_type=F32)


def partner(me, k, shards):
    out = 0
    for j in range(log2(shards)):
        bit = lax.rem(lax.div(me, 1 << j), 2)
        out = out + (1 - bit if (k >> j) & 1 else bit) * (1 << j)
    return out


def far_first(shards):
    order = []
    width = shards // 2
    while width:
        order += range(width, 2 * width)
        width //= 2
    return order


def kernel(
    shards, seg_ref, own_col_ref, own_row_ref, lscale_ref, rscale_ref, grad_hbm, left_hbm, right_hbm,
    out_hbm,
    p_own, p_got, wt, f, y_got, g, a, left_v, right_v, lperm, mid, u, ud, o, local_sem, send_sem, recv_sem,
):
    rep, me = lax.axis_index("rep"), lax.axis_index("shard")
    y, c = lax.rem(lax.div(rep, 2), 2), lax.rem(rep, 2)
    y_rep, c_rep = rep + 2 - 4 * y, rep + 1 - 2 * c
    blocks, order_b = seg_ref.shape
    rows = order_b // shards
    seg_local, half = p_own.shape
    flat = shards * rows
    order = far_first(shards)
    peers = {k: partner(me, k, shards) for k in order}
    here = pl.ds(pl.multiple_of(c * half, half), half)
    there = pl.ds(pl.multiple_of((1 - c) * half, half), half)

    loads = [
        pltpu.make_async_copy(grad_hbm.at[0, :, here], p_own, local_sem.at[0]),
        pltpu.make_async_copy(left_hbm.at[y], left_v, local_sem.at[1]),
    ]
    for i, r in enumerate((here, there)):
        for j, w in enumerate((here, there)):
            loads.append(pltpu.make_async_copy(
                right_hbm.at[y, r, w], right_v.at[i, :, pl.ds(j * half, half)], local_sem.at[2 + 2 * i + j]))
    for load in loads:
        load.start()

    def send(kind, k, src, dst, rep_to, shard_to):
        return pltpu.make_async_remote_copy(
            src_ref=src, dst_ref=dst, send_sem=send_sem.at[kind, k], recv_sem=recv_sem.at[kind, k],
            device_id={"rep": rep_to, "shard": shard_to}, device_id_type=MESH)

    barrier = pltpu.get_barrier_semaphore()
    pl.semaphore_signal(barrier, inc=1, device_id={"rep": c_rep, "shard": me}, device_id_type=MESH)
    pl.semaphore_signal(barrier, inc=1, device_id={"rep": y_rep, "shard": me}, device_id_type=MESH)
    for k in order:
        pl.semaphore_signal(barrier, inc=1, device_id={"rep": rep, "shard": peers[k]}, device_id_type=MESH)
    pl.semaphore_wait(barrier, 2 + len(order))

    pair = send(PAIR, 0, grad_hbm.at[0, :, there], p_got, c_rep, me)
    pair.start()

    seg = seg_ref[...]
    local = seg - me * seg_local
    local = jnp.where((local >= 0) & (local < seg_local), local, 0)
    digits = jnp.concatenate([local >> 4, local & 15], axis=0).astype(F32).astype(BF16)
    spread = one_hot((iota((order_b, flat), 0) >> log2(shards)) == (iota((order_b, flat), 1) & (rows - 1)))
    found = dot(digits, spread)
    place_of = found[:blocks] * 16.0 + found[blocks:] + 1.0
    own_col, own_row = own_col_ref[...], own_row_ref[...]
    earlier = iota((blocks, blocks), 1) < iota((blocks, blocks), 0)
    rank = jnp.sum(jnp.where((own_col == own_row) & earlier, 1.0, 0.0), axis=1, keepdims=True)
    key = own_col.astype(F32) * 2.0 + rank
    peer_row = (iota((1, flat), 1) >> log2(rows)) ^ me
    seg_id = iota((seg_local, flat), 0).astype(F32)
    for plane in range(2):
        wanted = (peer_row * 2 + lax.rem(y + plane, 2)).astype(F32)
        place = jnp.sum(jnp.where(key == wanted, place_of, 0.0), axis=0, keepdims=True) - 1.0
        wt[plane] = one_hot(seg_id == place)

    loads[0].wait()
    pair.wait_recv()
    q = (p_own[...].astype(F32) + p_got[...].astype(F32)).astype(BF16)
    f[1] = dot(wt[1], q, ((0,), (0,))).astype(BF16).reshape(shards, rows, half)
    y_out = {k: send(Y_OUT, k, f.at[1, k], y_got.at[k], y_rep, me) for k in order + [0]}
    for k in order + [0]:
        y_out[k].start()
    f[0] = dot(wt[0], q, ((0,), (0,))).astype(BF16).reshape(shards, rows, half)
    z_out = {k: send(Z_OUT, k, g.at[k], a.at[0, k], rep, peers[k]) for k in order}
    c_out = {k: send(C_OUT, k, a.at[0, k], a.at[1, k], c_rep, me) for k in order + [0]}
    for k in order + [0]:
        y_out[k].wait_recv()
        total = (f[0, k].astype(F32) + y_got[k].astype(F32)).astype(BF16)
        if k:
            g[k] = total
            z_out[k].start()
        else:
            a[0, 0] = total
            c_out[0].start()

    mine = key == (me * 2 + y).astype(F32)
    first = (seg[:, 0:1] >> log2(seg_local)).astype(F32)
    shift = jnp.sum(jnp.where(mine, first, 0.0), axis=0, keepdims=True).astype(jnp.int32)
    line = iota((flat, 1), 0)
    target = (line & (rows - 1)) * shards + ((((line >> log2(rows)) ^ me) - shift) & (shards - 1))
    chosen = iota((flat, order_b), 1) == target
    lscale = jnp.where(y == 0, lscale_ref[0:1, :], lscale_ref[1:2, :])
    lscale = jnp.sum(jnp.where(chosen, lscale, 0.0), axis=1, keepdims=True)
    rscale = jnp.where(y == 0, rscale_ref[0:1, :], rscale_ref[1:2, :])
    rscale = jnp.where(c == 0, rscale, jnp.concatenate([rscale[:, half:], rscale[:, :half]], axis=1))
    turn = one_hot(chosen)
    for load in loads[1:]:
        load.wait()
    lperm[...] = dot(dot(turn, left_v[...]).astype(BF16), turn, ((1,), (1,))).astype(BF16)

    for k in order:
        z_out[k].wait_recv()
        c_out[k].start()
    grad_power = jnp.zeros((1, 1), F32)
    near = shards // 2
    c_out[0].wait_recv()
    for low, high in ((near, shards), (0, near)):
        for k in range(max(low, 1), high):
            c_out[k].wait_recv()
        span = (high - low) * rows
        mine_half = a[0, low:high].reshape(span, half)
        other_half = a[1, low:high].reshape(span, half)
        part = dot(mine_half, right_v[0]) + dot(other_half, right_v[1])
        mid[low * rows:high * rows] = (part * rscale).astype(BF16)
        wide, wide_other = mine_half.astype(F32), other_half.astype(F32)
        grad_power += jnp.sum(wide * wide + wide_other * wide_other, keepdims=True)

    precond = dot(lperm[...], mid[...]) * lscale
    update_power = jnp.sum(precond * precond, keepdims=True)
    scale = 1.0 / (order_b * 2 * half)
    ratio = jnp.sqrt((grad_power * scale + EPSILON) / (update_power * scale + EPSILON))
    u[...] = (precond[:, :half] * ratio).astype(BF16).reshape(shards, rows, half)

    z_back = {k: send(Z_BACK, k, u.at[k], ud.at[0, 0, k], rep, peers[k]) for k in order}
    y_back = {k: send(Y_BACK, k, ud.at[0, 0, k], ud.at[1, 0, k], y_rep, me) for k in order + [0]}
    c_back = {k: send(C_BACK, k, ud.at[0, 0, k], ud.at[0, 1, k], c_rep, me) for k in order + [0]}
    c_far = {k: send(C_BACK_FAR, k, ud.at[1, 0, k], ud.at[1, 1, k], c_rep, me) for k in order + [0]}
    for k in order:
        z_back[k].start()
    ud[0, 0, 0] = u[0]
    arrivals = [0] + order
    for n in range(shards + 2):
        if n < shards:
            k = arrivals[n]
            if k:
                z_back[k].wait_recv()
            y_back[k].start()
            c_back[k].start()
        if n >= 2:
            k = arrivals[n - 2]
            y_back[k].wait_recv()
            c_far[k].start()

    def placed(side):
        return (dot(wt[0], ud[0, side].reshape(flat, half)) + dot(wt[1], ud[1, side].reshape(flat, half))).astype(BF16)

    o[0] = placed(0)
    write_own = pltpu.make_async_copy(o.at[0], out_hbm.at[:, here], local_sem.at[0])
    write_own.start()
    for k in arrivals:
        c_back[k].wait_recv()
        c_far[k].wait_recv()
    o[1] = placed(1)
    write_other = pltpu.make_async_copy(o.at[1], out_hbm.at[:, there], local_sem.at[1])
    write_other.start()
    pair.wait_send()
    for group in (y_out, z_out, c_out, z_back, y_back, c_back, c_far):
        for k in group:
            group[k].wait_send()
    write_own.wait()
    write_other.wait()


def on_device(grad_part, seg_slot, owner, left_code, left_scale, right_code, right_scale):
    shards, reps = lax.axis_size("shard"), lax.axis_size("rep")
    assert reps % 4 == 0 and left_code.shape[0] == 2
    if reps > 4:
        every = lax.all_gather(grad_part[0], "rep").astype(F32)
        sums = jnp.sum(every.reshape((reps // 4, 4) + every.shape[1:]), axis=0)
        grad_part = sums[lax.axis_index("rep") % 4][None].astype(BF16)
    _, seg_local, width = grad_part.shape
    half = width // 2
    blocks, order_b = seg_slot.shape
    rows = order_b // shards
    flat = shards * rows
    vmem = pl.BlockSpec(memory_space=pltpu.VMEM)
    hbm = pl.BlockSpec(memory_space=pl.ANY)
    return pl.pallas_call(
        functools.partial(kernel, shards),
        out_shape=jax.ShapeDtypeStruct((seg_local, width), BF16),
        in_specs=[vmem] * 5 + [hbm] * 3,
        out_specs=hbm,
        scratch_shapes=[
            pltpu.VMEM((seg_local, half), BF16),
            pltpu.VMEM((seg_local, half), BF16),
            pltpu.VMEM((2, seg_local, flat), BF16),
            pltpu.VMEM((2, shards, rows, half), BF16),
            pltpu.VMEM((shards, rows, half), BF16),
            pltpu.VMEM((shards, rows, half), BF16),
            pltpu.VMEM((2, shards, rows, half), BF16),
            pltpu.VMEM((order_b, order_b), BF16),
            pltpu.VMEM((2, half, width), BF16),
            pltpu.VMEM((flat, flat), BF16),
            pltpu.VMEM((flat, width), BF16),
            pltpu.VMEM((shards, rows, half), BF16),
            pltpu.VMEM((2, 2, shards, rows, half), BF16),
            pltpu.VMEM((2, seg_local, half), BF16),
            pltpu.SemaphoreType.DMA((6,)),
            pltpu.SemaphoreType.DMA((8, shards)),
            pltpu.SemaphoreType.DMA((8, shards)),
        ],
        compiler_params=pltpu.CompilerParams(
            collective_id=0, has_side_effects=True, vmem_limit_bytes=40 * 1024 * 1024
        ),
    )(seg_slot, owner[:, None], owner[None, :], left_scale, right_scale, grad_part, left_code, right_code)


def solution(mesh):
    in_specs = (
        P("rep", "shard", None),
        P(),
        P(),
        P("shard", None, None),
        P("shard", None),
        P("shard", None, None),
        P("shard", None),
    )
    out_specs = P("shard", None)
    return jax.shard_map(
        on_device, mesh=mesh, in_specs=in_specs, out_specs=out_specs, check_vma=False
    )
```

time: 152 us -> 45.3 us (0.30)
  waiting for transfers between devices: 78.6 us -> 0 us
  Pallas kernels: 0 us -> 38.6 us
  local copies, waits for them, and re-layouts: 41.3 us -> 6.42 us
  between operations: 13.5 us -> 0.02 us
  starting transfers between devices: 9.07 us -> 0 us
  other arithmetic: 5.69 us -> 0 us
  matrix products: 3.84 us -> 0 us
    all_to_all x2 -> x0, waiting for transfers between devices: 50.5 us -> none  [the longest x1 25.6 us: on_device(): lax.all_to_all(backward, 'shard', split_axis=0, concat_axis=0, tiled=True)]
    pallas_call x0 -> x1, Pallas kernels: none -> 38.6 us  [on_device(): pl.pallas_call(functools.partial(kernel, shards), out_shape=jax.ShapeDtyp...]
    gather x6 -> x0, local copies, waits for them, and re-layouts: 33.4 us -> none  [the longest x1 12.3 us: on_device(): update_block[jnp.arange(slot_count, dtype=jnp.int32)[None, :, None], dest...]
    psum x1 -> x0, waiting for transfers between devices: 27.4 us -> none  [on_device(): lax.psum(grad_part[0].astype(jnp.float32).astype(jnp.bfloat16), 'rep')]
    all_to_all x2 -> x0, starting transfers between devices: 9.07 us -> none  [the longest x1 5.51 us: on_device(): lax.all_to_all(outgoing, 'shard', split_axis=0, concat_axis=0, tiled=True)]
    scatter x1 -> x0, local copies, waits for them, and re-layouts: 5.78 us -> none  [on_device(): update.at[target.reshape(-1)]]
    unnamed x9 -> x15, local copies, waits for them, and re-layouts: 0.02 us -> 5.67 us
    dot_general x1 -> x0, matrix products: 3.84 us -> none  [on_device(): jnp.einsum('kij,kjl->kil', left_code, middle, preferred_element_type=jnp....]
  transfers between devices with their start and end apart: 3 -> 0, of which waited for: 3 -> 0; matrix products, arithmetic and copies ran while one was open for 7% -> 0% of each run, Pallas kernels for 0% -> 0%
where the time goes in v1:
time: 45.3 us; the launch traced here: 45 us
  Pallas kernels  38.6 us (85%)
  local copies, waits for them, and re-layouts  6.42 us (14%)
    pallas_call x1, Pallas kernels, on_device(): pl.pallas_call(functools.partial(kernel, shards), out_shape=jax.ShapeDtyp...  38.6 us
    unnamed x15, local copies, waits for them, and re-layouts  5.67 us

profile of v1, /device:TPU:0, one launch (start us, length us, event | category | flops | bytes accessed | tf_op | source)
XLA Modules:
  0.0 45.0 jit_solution(1369816085901229718)
XLA Ops:
  0.0 0.0 copy-start.5
  0.0 0.0 copy-start.4
  0.0 0.8 %copy.8.own_col_ref = s32[8,1]{1,0:T(8,128)S(1)} copy(s32[8,1]{0,1:T(1,128)} %bitcast.2) | data formatting | bytes 64 | tf_op jit(solution)/shard_map/broadcast_in_dim | solution.py:251
  0.8 0.0 copy-done.5
  0.8 0.0 copy-done.4
  0.8 0.0 copy-start
  0.8 1.2 %copy-done = bf16[2,512,512]{2,1,0:T(8,128)(2,1)S(1)} copy-done((bf16[2,512,512]{2,1,0:T(8,128)(2,1)S(1)}, bf16[2,512,512]{2,1,0:T(8,128)(2,1)}, u32[]{:S(2)}) %copy-start) | copy-done | bytes 1048600
  2.0 0.0 copy-start.1
  2.0 1.2 %copy-done.1 = bf16[2,512,512]{2,1,0:T(8,128)(2,1)S(1)} copy-done((bf16[2,512,512]{2,1,0:T(8,128)(2,1)S(1)}, bf16[2,512,512]{2,1,0:T(8,128)(2,1)}, u32[]{:S(2)}) %copy-start.1) | copy-done | bytes 1048600
  3.2 0.0 copy-start.2
  3.2 1.0 %copy-done.2 = bf16[1,512,512]{2,1,0:T(8,128)(2,1)S(1)} copy-done((bf16[1,512,512]{2,1,0:T(8,128)(2,1)S(1)}, bf16[1,512,512]{2,1,0:T(8,128)(2,1)}, u32[]{:S(2)}) %copy-start.2) | copy-done | bytes 524312
  4.3 0.0 copy-start.3
  4.3 0.7 %copy-done.3 = s32[8,512]{1,0:T(8,128)S(1)} copy-done((s32[8,512]{1,0:T(8,128)S(1)}, s32[8,512]{1,0:T(8,128)}, u32[]{:S(2)}) %copy-start.3) | copy-done | bytes 16408
  5.0 0.0 copy-start.6
  5.0 0.7 %copy-done.6 = s32[8]{0:T(128)S(1)} copy-done((s32[8]{0:T(128)S(1)}, s32[8]{0:T(128)}, u32[]{:S(2)}) %copy-start.6) | copy-done | bytes 56
  5.6 38.6 %shard_map.73 = bf16[512,512]{1,0:T(8,128)(2,1)S(1)} custom-call(s32[8,512]{1,0:T(8,128)S(1)} %copy-done.3, s32[8,1]{1,0:T(8,128)S(1)} %copy.8.own_col_ref, s32[1,8]{1,0:T(1,128)S(1)} %bitcast.3, f32[2,512]{1,0:T(2,128)S(1)} %copy-done.4, f32[2,512]{1,0:T(2,128)S(1)} %copy-done.5, bf16[1,512,512]{2,1,0:T(8,128)(2,1)S(1)} %copy-done.2, ...), custom_call_target="tpu_custom_call" | custom-call | tf_op jit(solution)/shard_map/pallas_call | solution.py:224
  44.2 0.8 %copy.10 = bf16[512,512]{1,0:T(8,128)(2,1)} copy(bf16[512,512]{1,0:T(8,128)(2,1)S(1)} %shard_map.73) | data formatting | bytes 1048576
Async XLA Ops:
  0.0 0.8 %copy-start.5 = (f32[2,512]{1,0:T(2,128)S(1)}, f32[2,512]{1,0:T(2,128)}, u32[]{:S(2)}) copy-start(f32[2,512]{1,0:T(2,128)} %rscale_ref.1) | copy-start | bytes 12292
  0.0 0.8 %copy-start.4 = (f32[2,512]{1,0:T(2,128)S(1)}, f32[2,512]{1,0:T(2,128)}, u32[]{:S(2)}) copy-start(f32[2,512]{1,0:T(2,128)} %lscale_ref.1) | copy-start | bytes 12292
  0.8 1.2 %copy-start = (bf16[2,512,512]{2,1,0:T(8,128)(2,1)S(1)}, bf16[2,512,512]{2,1,0:T(8,128)(2,1)}, u32[]{:S(2)}) copy-start(bf16[2,512,512]{2,1,0:T(8,128)(2,1)} %left_hbm.1) | copy-start | bytes 3145732
  2.0 1.2 %copy-start.1 = (bf16[2,512,512]{2,1,0:T(8,128)(2,1)S(1)}, bf16[2,512,512]{2,1,0:T(8,128)(2,1)}, u32[]{:S(2)}) copy-start(bf16[2,512,512]{2,1,0:T(8,128)(2,1)} %right_hbm.1) | copy-start | bytes 3145732
  3.2 1.0 %copy-start.2 = (bf16[1,512,512]{2,1,0:T(8,128)(2,1)S(1)}, bf16[1,512,512]{2,1,0:T(8,128)(2,1)}, u32[]{:S(2)}) copy-start(bf16[1,512,512]{2,1,0:T(8,128)(2,1)} %grad_hbm.1) | copy-start | bytes 1572868
  4.3 0.7 %copy-start.3 = (s32[8,512]{1,0:T(8,128)S(1)}, s32[8,512]{1,0:T(8,128)}, u32[]{:S(2)}) copy-start(s32[8,512]{1,0:T(8,128)} %seg_ref.1) | copy-start | bytes 49156
  5.0 0.7 %copy-start.6 = (s32[8]{0:T(128)S(1)}, s32[8]{0:T(128)}, u32[]{:S(2)}) copy-start(s32[8]{0:T(128)} %param.9) | copy-start | bytes 100

commit v2 on v1

--- a/solution.py
+++ b/solution.py
@@ -39,19 +39,19 @@
     return out
 
 
-def far_first(shards):
-    order = []
-    width = shards // 2
-    while width:
-        order += range(width, 2 * width)
-        width //= 2
+def send_order(shards):
+    far = list(range(shards // 2, shards))
+    near = [*range(shards // 4, shards // 2), *range(shards // 4 - 1, 0, -1)]
+    order = far[:2]
+    for n, k in enumerate(near):
+        order += [k] + far[n + 2:n + 3]
     return order
 
 
 def kernel(
-    shards, seg_ref, own_col_ref, own_row_ref, lscale_ref, rscale_ref, grad_hbm, left_hbm, right_hbm,
+    shards, seg_hbm, owner_hbm, lscale_hbm, rscale_hbm, grad_hbm, left_hbm, right_hbm,
     out_hbm,
-    p_own, p_got, wt, f, y_got, g, a, left_v, right_v, lperm, mid, u, ud, o, local_sem, send_sem, recv_sem,
+    seg_ref, owner_ref, lscale_ref, rscale_ref, p_own, p_got, wt, f, y_got, g, a, left_v, right_v, lperm, mid, u, ud, o, local_sem, send_sem, recv_sem,
 ):
     rep, me = lax.axis_index("rep"), lax.axis_index("shard")
     y, c = lax.rem(lax.div(rep, 2), 2), lax.rem(rep, 2)
@@ -60,11 +60,15 @@
     rows = order_b // shards
     seg_local, half = p_own.shape
     flat = shards * rows
-    order = far_first(shards)
+    order = send_order(shards)
     peers = {k: partner(me, k, shards) for k in order}
     here = pl.ds(pl.multiple_of(c * half, half), half)
     there = pl.ds(pl.multiple_of((1 - c) * half, half), half)
 
+    tables = [
+        pltpu.make_async_copy(seg_hbm, seg_ref, local_sem.at[6]),
+        pltpu.make_async_copy(owner_hbm, owner_ref, local_sem.at[7]),
+    ]
     loads = [
         pltpu.make_async_copy(grad_hbm.at[0, :, here], p_own, local_sem.at[0]),
         pltpu.make_async_copy(left_hbm.at[y], left_v, local_sem.at[1]),
@@ -73,8 +77,8 @@
         for j, w in enumerate((here, there)):
             loads.append(pltpu.make_async_copy(
                 right_hbm.at[y, r, w], right_v.at[i, :, pl.ds(j * half, half)], local_sem.at[2 + 2 * i + j]))
-    for load in loads:
-        load.start()
+    loads.append(pltpu.make_async_copy(lscale_hbm, lscale_ref, local_sem.at[8]))
+    loads.append(pltpu.make_async_copy(rscale_hbm, rscale_ref, local_sem.at[9]))
 
     def send(kind, k, src, dst, rep_to, shard_to):
         return pltpu.make_async_remote_copy(
@@ -86,22 +90,27 @@
     pl.semaphore_signal(barrier, inc=1, device_id={"rep": y_rep, "shard": me}, device_id_type=MESH)
     for k in order:
         pl.semaphore_signal(barrier, inc=1, device_id={"rep": rep, "shard": peers[k]}, device_id_type=MESH)
+    for load in tables + loads:
+        load.start()
+    spread = one_hot((iota((order_b, flat), 0) >> log2(shards)) == (iota((order_b, flat), 1) & (rows - 1)))
     pl.semaphore_wait(barrier, 2 + len(order))
 
     pair = send(PAIR, 0, grad_hbm.at[0, :, there], p_got, c_rep, me)
     pair.start()
 
+    for load in tables:
+        load.wait()
     seg = seg_ref[...]
     local = seg - me * seg_local
     local = jnp.where((local >= 0) & (local < seg_local), local, 0)
     digits = jnp.concatenate([local >> 4, local & 15], axis=0).astype(F32).astype(BF16)
-    spread = one_hot((iota((order_b, flat), 0) >> log2(shards)) == (iota((order_b, flat), 1) & (rows - 1)))
     found = dot(digits, spread)
     place_of = found[:blocks] * 16.0 + found[blocks:] + 1.0
-    own_col, own_row = own_col_ref[...], own_row_ref[...]
-    earlier = iota((blocks, blocks), 1) < iota((blocks, blocks), 0)
-    rank = jnp.sum(jnp.where((own_col == own_row) & earlier, 1.0, 0.0), axis=1, keepdims=True)
-    key = own_col.astype(F32) * 2.0 + rank
+    own_row = owner_ref[...].astype(F32)
+    line_b, lane_b = iota((blocks, blocks), 0), iota((blocks, blocks), 1)
+    own_col = jnp.sum(jnp.where(line_b == lane_b, own_row, 0.0), axis=1, keepdims=True)
+    rank = jnp.sum(jnp.where((own_col == own_row) & (lane_b < line_b), 1.0, 0.0), axis=1, keepdims=True)
+    key = own_col * 2.0 + rank
     peer_row = (iota((1, flat), 1) >> log2(rows)) ^ me
     seg_id = iota((seg_local, flat), 0).astype(F32)
     for plane in range(2):
@@ -119,7 +128,8 @@
     f[0] = dot(wt[0], q, ((0,), (0,))).astype(BF16).reshape(shards, rows, half)
     z_out = {k: send(Z_OUT, k, g.at[k], a.at[0, k], rep, peers[k]) for k in order}
     c_out = {k: send(C_OUT, k, a.at[0, k], a.at[1, k], c_rep, me) for k in order + [0]}
-    for k in order + [0]:
+
+    def pass_on(k):
         y_out[k].wait_recv()
         total = (f[0, k].astype(F32) + y_got[k].astype(F32)).astype(BF16)
         if k:
@@ -129,6 +139,11 @@
             a[0, 0] = total
             c_out[0].start()
 
+    for k in order[:shards // 2]:
+        pass_on(k)
+
+    for load in loads[1:]:
+        load.wait()
     mine = key == (me * 2 + y).astype(F32)
     first = (seg[:, 0:1] >> log2(seg_local)).astype(F32)
     shift = jnp.sum(jnp.where(mine, first, 0.0), axis=0, keepdims=True).astype(jnp.int32)
@@ -140,18 +155,19 @@
     rscale = jnp.where(y == 0, rscale_ref[0:1, :], rscale_ref[1:2, :])
     rscale = jnp.where(c == 0, rscale, jnp.concatenate([rscale[:, half:], rscale[:, :half]], axis=1))
     turn = one_hot(chosen)
-    for load in loads[1:]:
-        load.wait()
     lperm[...] = dot(dot(turn, left_v[...]).astype(BF16), turn, ((1,), (1,))).astype(BF16)
 
-    for k in order:
-        z_out[k].wait_recv()
-        c_out[k].start()
+    for k in order[shards // 2:] + [0]:
+        pass_on(k)
     grad_power = jnp.zeros((1, 1), F32)
-    near = shards // 2
-    c_out[0].wait_recv()
-    for low, high in ((near, shards), (0, near)):
-        for k in range(max(low, 1), high):
+    quarter = shards // 4
+    waiting = list(order)
+    for low, high in ((quarter, 3 * quarter), (0, quarter), (3 * quarter, shards)):
+        while any(low <= k < high for k in waiting):
+            k = waiting.pop(0)
+            z_out[k].wait_recv()
+            c_out[k].start()
+        for k in range(low, high):
             c_out[k].wait_recv()
         span = (high - low) * rows
         mine_half = a[0, low:high].reshape(span, half)
@@ -175,15 +191,16 @@
         z_back[k].start()
     ud[0, 0, 0] = u[0]
     arrivals = [0] + order
-    for n in range(shards + 2):
+    lag = 3
+    for n in range(shards + lag):
         if n < shards:
             k = arrivals[n]
             if k:
                 z_back[k].wait_recv()
             y_back[k].start()
             c_back[k].start()
-        if n >= 2:
-            k = arrivals[n - 2]
+        if n >= lag:
+            k = arrivals[n - lag]
             y_back[k].wait_recv()
             c_far[k].start()
 
@@ -219,14 +236,17 @@
     blocks, order_b = seg_slot.shape
     rows = order_b // shards
     flat = shards * rows
-    vmem = pl.BlockSpec(memory_space=pltpu.VMEM)
-    hbm = pl.BlockSpec(memory_space=pl.ANY)
+    hbm = pl.BlockSpec(memory_space=pltpu.HBM)
     return pl.pallas_call(
         functools.partial(kernel, shards),
         out_shape=jax.ShapeDtypeStruct((seg_local, width), BF16),
-        in_specs=[vmem] * 5 + [hbm] * 3,
+        in_specs=[hbm] * 7,
         out_specs=hbm,
         scratch_shapes=[
+            pltpu.VMEM((blocks, order_b), jnp.int32),
+            pltpu.VMEM((1, blocks), jnp.int32),
+            pltpu.VMEM((2, order_b), F32),
+            pltpu.VMEM((2, width), F32),
             pltpu.VMEM((seg_local, half), BF16),
             pltpu.VMEM((seg_local, half), BF16),
             pltpu.VMEM((2, seg_local, flat), BF16),
@@ -241,14 +261,14 @@
             pltpu.VMEM((shards, rows, half), BF16),
             pltpu.VMEM((2, 2, shards, rows, half), BF16),
             pltpu.VMEM((2, seg_local, half), BF16),
-            pltpu.SemaphoreType.DMA((6,)),
+            pltpu.SemaphoreType.DMA((10,)),
             pltpu.SemaphoreType.DMA((8, shards)),
             pltpu.SemaphoreType.DMA((8, shards)),
         ],
         compiler_params=pltpu.CompilerParams(
-            collective_id=0, has_side_effects=True, vmem_limit_bytes=40 * 1024 * 1024
+            collective_id=0, has_side_effects=True, vmem_limit_bytes=60 * 1024 * 1024
         ),
-    )(seg_slot, owner[:, None], owner[None, :], left_scale, right_scale, grad_part, left_code, right_code)
+    )(seg_slot, owner[None, :], left_scale, right_scale, grad_part, left_code, right_code)
 
 
 def solution(mesh):

time: 45.3 us -> 39.7 us (0.88)
  local copies, waits for them, and re-layouts: 6.42 us -> 1.87 us
  Pallas kernels: 38.6 us -> 37.6 us
    unnamed x15 -> x1, local copies, waits for them, and re-layouts: 5.67 us -> 1.87 us
    pallas_call x1, Pallas kernels: 38.6 us -> 37.6 us  [on_device(): pl.pallas_call(functools.partial(kernel, shards), out_shape=jax.ShapeDtyp...]
    broadcast_in_dim x1 -> x0, local copies, waits for them, and re-layouts: 0.76 us -> none  [on_device(): owner[:, None]]
where the time goes in v2:
time: 39.7 us; the launch traced here: 39.5 us
  Pallas kernels  37.6 us (95%)
  local copies, waits for them, and re-layouts  1.87 us (5%)
    pallas_call x1, Pallas kernels, on_device(): pl.pallas_call(functools.partial(kernel, shards), out_shape=jax.ShapeDtyp...  37.6 us
    unnamed x1, local copies, waits for them, and re-layouts  1.87 us

profile of v2, /device:TPU:0, one launch (start us, length us, event | category | flops | bytes accessed | tf_op | source)
XLA Modules:
  0.0 39.5 jit_solution(9101495750879281088)
XLA Ops:
  0.0 37.6 %shard_map.73 = bf16[512,512]{1,0:T(8,128)(2,1)} custom-call(s32[8,512]{1,0:T(8,128)} %seg_hbm.1, s32[1,8]{1,0:T(1,128)} %bitcast.1, f32[2,512]{1,0:T(2,128)} %lscale_hbm.1, f32[2,512]{1,0:T(2,128)} %rscale_hbm.1, bf16[1,512,512]{2,1,0:T(8,128)(2,1)} %grad_hbm.1, bf16[2,512,512]{2,1,0:T(8,128)(2,1)} %left_hbm.1, bf16[2,512,512]{2,1,0:T(8,128)(2,1)} %right_hbm.1), custom_call_target="tpu_custom_call" | custom-call | tf_op jit(solution)/shard_map/pallas_call | solution.py:240
  37.7 1.9 %copy.9 = bf16[512,512]{1,0:T(8,128)(2,1)} copy(bf16[512,512]{1,0:T(8,128)(2,1)} %shard_map.73) | data formatting | bytes 1048576

commit v3 on v2

--- a/solution.py
+++ b/solution.py
@@ -11,7 +11,7 @@
 MESH = pl.DeviceIdType.MESH
 F32 = jnp.float32
 BF16 = jnp.bfloat16
-Y_OUT, Z_OUT, C_OUT, Z_BACK, Y_BACK, C_BACK, C_BACK_FAR, PAIR = range(8)
+Y_OUT, Z_OUT, C_OUT, Z_BACK, Y_BACK, C_BACK, PAIR = range(7)
 
 
 def log2(value):
@@ -50,8 +50,8 @@
 
 def kernel(
     shards, seg_hbm, owner_hbm, lscale_hbm, rscale_hbm, grad_hbm, left_hbm, right_hbm,
-    out_hbm,
-    seg_ref, owner_ref, lscale_ref, rscale_ref, p_own, p_got, wt, f, y_got, g, a, left_v, right_v, lperm, mid, u, ud, o, local_sem, send_sem, recv_sem,
+    own_hbm, other_hbm,
+    seg_ref, owner_ref, lscale_ref, rscale_ref, p_own, p_got, wt, f, y_got, g, a, left_v, right_v, lperm, mid, u, ud, acc, done, local_sem, send_sem, recv_sem,
 ):
     rep, me = lax.axis_index("rep"), lax.axis_index("shard")
     y, c = lax.rem(lax.div(rep, 2), 2), lax.rem(rep, 2)
@@ -127,7 +127,11 @@
         y_out[k].start()
     f[0] = dot(wt[0], q, ((0,), (0,))).astype(BF16).reshape(shards, rows, half)
     z_out = {k: send(Z_OUT, k, g.at[k], a.at[0, k], rep, peers[k]) for k in order}
-    c_out = {k: send(C_OUT, k, a.at[0, k], a.at[1, k], c_rep, me) for k in order + [0]}
+    quarter = shards // 4
+    spans = ((quarter, 3 * quarter), (0, quarter), (3 * quarter, shards))
+    c_out = {
+        n: send(C_OUT, n, a.at[0, low:high], a.at[1, low:high], c_rep, me) for n, (low, high) in enumerate(spans)
+    }
 
     def pass_on(k):
         y_out[k].wait_recv()
@@ -137,7 +141,6 @@
             z_out[k].start()
         else:
             a[0, 0] = total
-            c_out[0].start()
 
     for k in order[:shards // 2]:
         pass_on(k)
@@ -160,15 +163,13 @@
     for k in order[shards // 2:] + [0]:
         pass_on(k)
     grad_power = jnp.zeros((1, 1), F32)
-    quarter = shards // 4
     waiting = list(order)
-    for low, high in ((quarter, 3 * quarter), (0, quarter), (3 * quarter, shards)):
+    for n, (low, high) in enumerate(spans):
         while any(low <= k < high for k in waiting):
-            k = waiting.pop(0)
-            z_out[k].wait_recv()
-            c_out[k].start()
-        for k in range(low, high):
-            c_out[k].wait_recv()
+            z_out[waiting.pop(0)].wait_recv()
+        c_out[n].start()
+    for n, (low, high) in enumerate(spans):
+        c_out[n].wait_recv()
         span = (high - low) * rows
         mine_half = a[0, low:high].reshape(span, half)
         other_half = a[1, low:high].reshape(span, half)
@@ -183,45 +184,44 @@
     ratio = jnp.sqrt((grad_power * scale + EPSILON) / (update_power * scale + EPSILON))
     u[...] = (precond[:, :half] * ratio).astype(BF16).reshape(shards, rows, half)
 
-    z_back = {k: send(Z_BACK, k, u.at[k], ud.at[0, 0, k], rep, peers[k]) for k in order}
-    y_back = {k: send(Y_BACK, k, ud.at[0, 0, k], ud.at[1, 0, k], y_rep, me) for k in order + [0]}
-    c_back = {k: send(C_BACK, k, ud.at[0, 0, k], ud.at[0, 1, k], c_rep, me) for k in order + [0]}
-    c_far = {k: send(C_BACK_FAR, k, ud.at[1, 0, k], ud.at[1, 1, k], c_rep, me) for k in order + [0]}
+    z_back = {k: send(Z_BACK, k, u.at[k], ud.at[0, k], rep, peers[k]) for k in order}
+    y_back = {k: send(Y_BACK, k, ud.at[0, k], ud.at[1, k], y_rep, me) for k in order + [0]}
     for k in order:
         z_back[k].start()
-    ud[0, 0, 0] = u[0]
-    arrivals = [0] + order
-    lag = 3
-    for n in range(shards + lag):
-        if n < shards:
-            k = arrivals[n]
-            if k:
-                z_back[k].wait_recv()
-            y_back[k].start()
-            c_back[k].start()
-        if n >= lag:
-            k = arrivals[n - lag]
-            y_back[k].wait_recv()
-            c_far[k].start()
-
-    def placed(side):
-        return (dot(wt[0], ud[0, side].reshape(flat, half)) + dot(wt[1], ud[1, side].reshape(flat, half))).astype(BF16)
-
-    o[0] = placed(0)
-    write_own = pltpu.make_async_copy(o.at[0], out_hbm.at[:, here], local_sem.at[0])
-    write_own.start()
-    for k in arrivals:
-        c_back[k].wait_recv()
-        c_far[k].wait_recv()
-    o[1] = placed(1)
-    write_other = pltpu.make_async_copy(o.at[1], out_hbm.at[:, there], local_sem.at[1])
-    write_other.start()
+    ud[0, 0] = u[0]
+    y_back[0].start()
+    for k in order:
+        z_back[k].wait_recv()
+        y_back[k].start()
+
+    def placed(at, low, high):
+        lanes = slice(low * rows, high * rows)
+        span = (high - low) * rows
+        return sum(dot(wt[n, at, lanes], ud[n, low:high].reshape(span, half)) for n in range(2))
+
+    waiting = [0] + order
+    low, high = spans[0]
+    while any(low <= k < high for k in waiting):
+        y_back[waiting.pop(0)].wait_recv()
+    acc[...] = placed(slice(None), low, high)
+    for k in waiting:
+        y_back[k].wait_recv()
+    c_back, writes = {}, []
+    for n in range(2):
+        at = slice(n * seg_local // 2, (n + 1) * seg_local // 2)
+        done[at] = (acc[at] + placed(at, *spans[1]) + placed(at, *spans[2])).astype(BF16)
+        c_back[n] = send(C_BACK, n, done.at[at], other_hbm.at[at], c_rep, me)
+        c_back[n].start()
+        writes.append(pltpu.make_async_copy(done.at[at], own_hbm.at[at], local_sem.at[n]))
+        writes[n].start()
+    for n in c_back:
+        c_back[n].wait_recv()
     pair.wait_send()
-    for group in (y_out, z_out, c_out, z_back, y_back, c_back, c_far):
+    for group in (y_out, z_out, c_out, z_back, y_back, c_back):
         for k in group:
             group[k].wait_send()
-    write_own.wait()
-    write_other.wait()
+    for write in writes:
+        write.wait()
 
 
 def on_device(grad_part, seg_slot, owner, left_code, left_scale, right_code, right_scale):
@@ -237,11 +237,11 @@
     rows = order_b // shards
     flat = shards * rows
     hbm = pl.BlockSpec(memory_space=pltpu.HBM)
-    return pl.pallas_call(
+    own, other = pl.pallas_call(
         functools.partial(kernel, shards),
-        out_shape=jax.ShapeDtypeStruct((seg_local, width), BF16),
+        out_shape=[jax.ShapeDtypeStruct((seg_local, half), BF16)] * 2,
         in_specs=[hbm] * 7,
-        out_specs=hbm,
+        out_specs=[hbm, hbm],
         scratch_shapes=[
             pltpu.VMEM((blocks, order_b), jnp.int32),
             pltpu.VMEM((1, blocks), jnp.int32),
@@ -259,16 +259,19 @@
             pltpu.VMEM((flat, flat), BF16),
             pltpu.VMEM((flat, width), BF16),
             pltpu.VMEM((shards, rows, half), BF16),
-            pltpu.VMEM((2, 2, shards, rows, half), BF16),
-            pltpu.VMEM((2, seg_local, half), BF16),
+            pltpu.VMEM((2, shards, rows, half), BF16),
+            pltpu.VMEM((seg_local, half), F32),
+            pltpu.VMEM((seg_local, half), BF16),
             pltpu.SemaphoreType.DMA((10,)),
-            pltpu.SemaphoreType.DMA((8, shards)),
-            pltpu.SemaphoreType.DMA((8, shards)),
+            pltpu.SemaphoreType.DMA((7, shards)),
+            pltpu.SemaphoreType.DMA((7, shards)),
         ],
         compiler_params=pltpu.CompilerParams(
             collective_id=0, has_side_effects=True, vmem_limit_bytes=60 * 1024 * 1024
         ),
     )(seg_slot, owner[None, :], left_scale, right_scale, grad_part, left_code, right_code)
+    first = (lax.axis_index("rep") & 1) == 0
+    return jnp.concatenate([jnp.where(first, own, other), jnp.where(first, other, own)], axis=1)
 
 
 def solution(mesh):

time: 39.7 us -> 37.6 us (0.947)
  Pallas kernels: 37.6 us -> 35.5 us
  other arithmetic: 0 us -> 1.9 us
  local copies, waits for them, and re-layouts: 1.87 us -> 0 us
    pallas_call x1, Pallas kernels: 37.6 us -> 35.5 us  [on_device(): pl.pallas_call(functools.partial(kernel, shards), out_shape=[jax.ShapeDty...]
    unnamed x1 -> x0, local copies, waits for them, and re-layouts: 1.87 us -> none
    select_n x0 -> x1, other arithmetic: none -> 1.07 us  [on_device(): jnp.where(first, own, other)]
    concatenate x0 -> x1, other arithmetic: none -> 0.83 us  [on_device(): jnp.concatenate([jnp.where(first, own, other), jnp.where(first, other, ow...]
where the time goes in v3:
time: 37.6 us; the launch traced here: 37.4 us
  Pallas kernels  35.5 us (94%)
  other arithmetic  1.9 us (5%)
    pallas_call x1, Pallas kernels, on_device(): pl.pallas_call(functools.partial(kernel, shards), out_shape=[jax.ShapeDty...  35.5 us
    select_n x1, other arithmetic, on_device(): jnp.where(first, own, other)  1.07 us
    concatenate x1, other arithmetic, on_device(): jnp.concatenate([jnp.where(first, own, other), jnp.where(first, other, ow...  0.83 us

profile of v3, /device:TPU:0, one launch (start us, length us, event | category | flops | bytes accessed | tf_op | source)
XLA Modules:
  0.0 37.4 jit_solution(10295462899666371648)
XLA Ops:
  0.0 35.5 %shard_map.73 = (bf16[512,256]{1,0:T(8,128)(2,1)}, bf16[512,256]{1,0:T(8,128)(2,1)}) custom-call(s32[8,512]{1,0:T(8,128)} %seg_hbm.1, s32[1,8]{1,0:T(1,128)} %bitcast.1, f32[2,512]{1,0:T(2,128)} %lscale_hbm.1, f32[2,512]{1,0:T(2,128)} %rscale_hbm.1, bf16[1,512,512]{2,1,0:T(8,128)(2,1)} %grad_hbm.1, bf16[2,512,512]{2,1,0:T(8,128)(2,1)} %left_hbm.1, ...), custom_call_target="tpu_custom_call" | custom-call | tf_op jit(solution)/shard_map/pallas_call | solution.py:240
  35.5 1.1 %broadcast_select_fusion.1 = (bf16[512,256]{1,0:T(8,128)(2,1)S(1)}, bf16[512,256]{1,0:T(8,128)(2,1)S(1)}) fusion(bf16[512,256]{1,0:T(8,128)(2,1)} %get-tuple-element.7, bf16[512,256]{1,0:T(8,128)(2,1)} %get-tuple-element.8, pred[]{:T(512)S(6)} %eq.3), kind=kLoop, calls=%fused_computation.2 | loop fusion | flops 262144 | bytes 1048577 | tf_op jit(solution)/shard_map/jit(_where)/select_n | solution.py:274
  36.6 0.8 %pad_maximum_fusion = bf16[512,512]{1,0:T(8,128)(2,1)} fusion(bf16[512,256]{1,0:T(8,128)(2,1)S(1)} %get-tuple-element.10, bf16[512,256]{1,0:T(8,128)(2,1)S(1)} %get-tuple-element.9), kind=kLoop, calls=%fused_computation | loop fusion | flops 1048576 | bytes 1048576 | tf_op jit(solution)/shard_map/concatenate | solution.py:274

commit v4 on v3

--- a/solution.py
+++ b/solution.py
@@ -12,6 +12,7 @@
 F32 = jnp.float32
 BF16 = jnp.bfloat16
 Y_OUT, Z_OUT, C_OUT, Z_BACK, Y_BACK, C_BACK, PAIR = range(7)
+JOINS = 4
 
 
 def log2(value):
@@ -92,7 +93,7 @@
         pl.semaphore_signal(barrier, inc=1, device_id={"rep": rep, "shard": peers[k]}, device_id_type=MESH)
     for load in tables + loads:
         load.start()
-    spread = one_hot((iota((order_b, flat), 0) >> log2(shards)) == (iota((order_b, flat), 1) & (rows - 1)))
+    gather = one_hot((iota((flat, order_b), 1) >> log2(shards)) == (iota((flat, order_b), 0) & (rows - 1)))
     pl.semaphore_wait(barrier, 2 + len(order))
 
     pair = send(PAIR, 0, grad_hbm.at[0, :, there], p_got, c_rep, me)
@@ -104,28 +105,31 @@
     local = seg - me * seg_local
     local = jnp.where((local >= 0) & (local < seg_local), local, 0)
     digits = jnp.concatenate([local >> 4, local & 15], axis=0).astype(F32).astype(BF16)
-    found = dot(digits, spread)
-    place_of = found[:blocks] * 16.0 + found[blocks:] + 1.0
+    found = dot(gather, digits, ((1,), (1,)))
+    place_of = found[:, :blocks] * 16.0 + found[:, blocks:] + 1.0
     own_row = owner_ref[...].astype(F32)
     line_b, lane_b = iota((blocks, blocks), 0), iota((blocks, blocks), 1)
     own_col = jnp.sum(jnp.where(line_b == lane_b, own_row, 0.0), axis=1, keepdims=True)
-    rank = jnp.sum(jnp.where((own_col == own_row) & (lane_b < line_b), 1.0, 0.0), axis=1, keepdims=True)
-    key = own_col * 2.0 + rank
-    peer_row = (iota((1, flat), 1) >> log2(rows)) ^ me
-    seg_id = iota((seg_local, flat), 0).astype(F32)
-    for plane in range(2):
-        wanted = (peer_row * 2 + lax.rem(y + plane, 2)).astype(F32)
-        place = jnp.sum(jnp.where(key == wanted, place_of, 0.0), axis=0, keepdims=True) - 1.0
-        wt[plane] = one_hot(seg_id == place)
-
+    same = own_col == own_row
+    key_row = own_row * 2.0 + jnp.sum(jnp.where(same & (line_b < lane_b), 1.0, 0.0), axis=0, keepdims=True)
+    key = own_col * 2.0 + jnp.sum(jnp.where(same & (lane_b < line_b), 1.0, 0.0), axis=1, keepdims=True)
+    peer_col = (iota((flat, 1), 0) >> log2(rows)) ^ me
+    seg_lane = iota((flat, seg_local), 1).astype(F32)
+
+    def picked(plane):
+        wanted = (peer_col * 2 + lax.rem(y + plane, 2)).astype(F32)
+        place = jnp.sum(jnp.where(key_row == wanted, place_of, 0.0), axis=1, keepdims=True) - 1.0
+        return one_hot(seg_lane == place)
+
+    pick_far = picked(1)
     loads[0].wait()
     pair.wait_recv()
     q = (p_own[...].astype(F32) + p_got[...].astype(F32)).astype(BF16)
-    f[1] = dot(wt[1], q, ((0,), (0,))).astype(BF16).reshape(shards, rows, half)
+    f[1] = dot(pick_far, q).astype(BF16).reshape(shards, rows, half)
     y_out = {k: send(Y_OUT, k, f.at[1, k], y_got.at[k], y_rep, me) for k in order + [0]}
     for k in order + [0]:
         y_out[k].start()
-    f[0] = dot(wt[0], q, ((0,), (0,))).astype(BF16).reshape(shards, rows, half)
+    f[0] = dot(picked(0), q).astype(BF16).reshape(shards, rows, half)
     z_out = {k: send(Z_OUT, k, g.at[k], a.at[0, k], rep, peers[k]) for k in order}
     quarter = shards // 4
     spans = ((quarter, 3 * quarter), (0, quarter), (3 * quarter, shards))
@@ -144,6 +148,16 @@
 
     for k in order[:shards // 2]:
         pass_on(k)
+
+    spread = one_hot((iota((order_b, flat), 0) >> log2(shards)) == (iota((order_b, flat), 1) & (rows - 1)))
+    found = dot(digits, spread)
+    place_of = found[:blocks] * 16.0 + found[blocks:] + 1.0
+    peer_row = (iota((1, flat), 1) >> log2(rows)) ^ me
+    seg_id = iota((seg_local, flat), 0).astype(F32)
+    for plane in range(2):
+        wanted = (peer_row * 2 + lax.rem(y + plane, 2)).astype(F32)
+        place = jnp.sum(jnp.where(key == wanted, place_of, 0.0), axis=0, keepdims=True) - 1.0
+        wt[plane] = one_hot(seg_id == place)
 
     for load in loads[1:]:
         load.wait()
@@ -162,13 +176,11 @@
 
     for k in order[shards // 2:] + [0]:
         pass_on(k)
-    grad_power = jnp.zeros((1, 1), F32)
-    waiting = list(order)
-    for n, (low, high) in enumerate(spans):
-        while any(low <= k < high for k in waiting):
-            z_out[waiting.pop(0)].wait_recv()
-        c_out[n].start()
-    for n, (low, high) in enumerate(spans):
+    late = order[:-2] + [order[-1], order[-2]]
+    waiting = list(late)
+
+    def middle(n):
+        low, high = spans[n]
         c_out[n].wait_recv()
         span = (high - low) * rows
         mine_half = a[0, low:high].reshape(span, half)
@@ -176,7 +188,16 @@
         part = dot(mine_half, right_v[0]) + dot(other_half, right_v[1])
         mid[low * rows:high * rows] = (part * rscale).astype(BF16)
         wide, wide_other = mine_half.astype(F32), other_half.astype(F32)
-        grad_power += jnp.sum(wide * wide + wide_other * wide_other, keepdims=True)
+        return jnp.sum(wide * wide + wide_other * wide_other, keepdims=True)
+
+    grad_power = jnp.zeros((1, 1), F32)
+    for n, (low, high) in enumerate(spans):
+        while any(low <= k < high for k in waiting):
+            z_out[waiting.pop(0)].wait_recv()
+        c_out[n].start()
+        if n:
+            grad_power += middle(n - 1)
+    grad_power += middle(len(spans) - 1)
 
     precond = dot(lperm[...], mid[...]) * lscale
     update_power = jnp.sum(precond * precond, keepdims=True)
@@ -190,7 +211,7 @@
         z_back[k].start()
     ud[0, 0] = u[0]
     y_back[0].start()
-    for k in order:
+    for k in late:
         z_back[k].wait_recv()
         y_back[k].start()
 
@@ -199,7 +220,7 @@
         span = (high - low) * rows
         return sum(dot(wt[n, at, lanes], ud[n, low:high].reshape(span, half)) for n in range(2))
 
-    waiting = [0] + order
+    waiting = [0] + late
     low, high = spans[0]
     while any(low <= k < high for k in waiting):
         y_back[waiting.pop(0)].wait_recv()
@@ -222,6 +243,22 @@
             group[k].wait_send()
     for write in writes:
         write.wait()
+
+
+def join(own_hbm, other_hbm, out_hbm, sem):
+    c = lax.rem(lax.axis_index("rep"), 2)
+    seg_local, half = own_hbm.shape
+    step = seg_local // JOINS
+    copies = []
+    for n, (ref, side) in enumerate(((own_hbm, c), (other_hbm, 1 - c))):
+        lanes = pl.ds(pl.multiple_of(side * half, half), half)
+        for i in range(JOINS):
+            at = pl.ds(i * step, step)
+            copies.append(pltpu.make_async_copy(ref.at[at], out_hbm.at[at, lanes], sem.at[n, i]))
+    for copy in copies:
+        copy.start()
+    for copy in copies:
+        copy.wait()
 
 
 def on_device(grad_part, seg_slot, owner, left_code, left_scale, right_code, right_scale):
@@ -270,8 +307,14 @@
             collective_id=0, has_side_effects=True, vmem_limit_bytes=60 * 1024 * 1024
         ),
     )(seg_slot, owner[None, :], left_scale, right_scale, grad_part, left_code, right_code)
-    first = (lax.axis_index("rep") & 1) == 0
-    return jnp.concatenate([jnp.where(first, own, other), jnp.where(first, other, own)], axis=1)
+    return pl.pallas_call(
+        join,
+        out_shape=jax.ShapeDtypeStruct((seg_local, width), BF16),
+        in_specs=[hbm, hbm],
+        out_specs=hbm,
+        scratch_shapes=[pltpu.SemaphoreType.DMA((2, JOINS))],
+        compiler_params=pltpu.CompilerParams(vmem_limit_bytes=60 * 1024 * 1024),
+    )(own, other)
 
 
 def solution(mesh):

time: 37.6 us -> 52 us (1.38)
  Pallas kernels: 35.5 us -> 51.8 us
  other arithmetic: 1.9 us -> 0 us
    pallas_call x0 -> x1, Pallas kernels: none -> 17.1 us  [on_device(): pl.pallas_call(join, out_shape=jax.ShapeDtypeStruct((seg_local, width), B...]
    select_n x1 -> x0, other arithmetic: 1.07 us -> none  [on_device(): jnp.where(first, own, other)]
    concatenate x1 -> x0, other arithmetic: 0.83 us -> none  [on_device(): jnp.concatenate([jnp.where(first, own, other), jnp.where(first, other, ow...]
    pallas_call x1, Pallas kernels: 35.5 us -> 34.7 us  [on_device(): pl.pallas_call(functools.partial(kernel, shards), out_shape=[jax.ShapeDty...]
where the time goes in v4:
time: 52 us; the launch traced here: 51.8 us
  Pallas kernels  51.8 us (100%)
    pallas_call x1, Pallas kernels, on_device(): pl.pallas_call(functools.partial(kernel, shards), out_shape=[jax.ShapeDty...  34.7 us
    pallas_call x1, Pallas kernels, on_device(): pl.pallas_call(join, out_shape=jax.ShapeDtypeStruct((seg_local, width), B...  17.1 us

profile of v4, /device:TPU:0, one launch (start us, length us, event | category | flops | bytes accessed | tf_op | source)
XLA Modules:
  0.0 51.8 jit_solution(12636332969180425885)
XLA Ops:
  0.0 34.7 %shard_map.73 = (bf16[512,256]{1,0:T(8,128)(2,1)}, bf16[512,256]{1,0:T(8,128)(2,1)}) custom-call(s32[8,512]{1,0:T(8,128)} %seg_hbm.1, s32[1,8]{1,0:T(1,128)} %bitcast.1, f32[2,512]{1,0:T(2,128)} %lscale_hbm.1, f32[2,512]{1,0:T(2,128)} %rscale_hbm.1, bf16[1,512,512]{2,1,0:T(8,128)(2,1)} %grad_hbm.1, bf16[2,512,512]{2,1,0:T(8,128)(2,1)} %left_hbm.1, ...), custom_call_target="tpu_custom_call" | custom-call | tf_op jit(solution)/shard_map/pallas_call | solution.py:277
  34.8 17.1 %shard_map.74 = bf16[512,512]{1,0:T(8,128)(2,1)} custom-call(bf16[512,256]{1,0:T(8,128)(2,1)} %get-tuple-element.7.own_hbm, bf16[512,256]{1,0:T(8,128)(2,1)} %get-tuple-element.8.other_hbm), custom_call_target="tpu_custom_call" | custom-call | tf_op jit(solution)/shard_map/pallas_call | solution.py:310

commit v5 on v4

--- a/solution.py
+++ b/solution.py
@@ -86,18 +86,20 @@
             src_ref=src, dst_ref=dst, send_sem=send_sem.at[kind, k], recv_sem=recv_sem.at[kind, k],
             device_id={"rep": rep_to, "shard": shard_to}, device_id_type=MESH)
 
+    for load in tables + loads[:1]:
+        load.start()
     barrier = pltpu.get_barrier_semaphore()
     pl.semaphore_signal(barrier, inc=1, device_id={"rep": c_rep, "shard": me}, device_id_type=MESH)
     pl.semaphore_signal(barrier, inc=1, device_id={"rep": y_rep, "shard": me}, device_id_type=MESH)
     for k in order:
         pl.semaphore_signal(barrier, inc=1, device_id={"rep": rep, "shard": peers[k]}, device_id_type=MESH)
-    for load in tables + loads:
+    pl.semaphore_wait(barrier, 2 + len(order))
+
+    pair = send(PAIR, 0, grad_hbm.at[0, :, there], p_got, c_rep, me)
+    pair.start()
+    for load in loads[1:]:
         load.start()
     gather = one_hot((iota((flat, order_b), 1) >> log2(shards)) == (iota((flat, order_b), 0) & (rows - 1)))
-    pl.semaphore_wait(barrier, 2 + len(order))
-
-    pair = send(PAIR, 0, grad_hbm.at[0, :, there], p_got, c_rep, me)
-    pair.start()
 
     for load in tables:
         load.wait()
@@ -146,18 +148,8 @@
         else:
             a[0, 0] = total
 
-    for k in order[:shards // 2]:
+    for k in order[:-1]:
         pass_on(k)
-
-    spread = one_hot((iota((order_b, flat), 0) >> log2(shards)) == (iota((order_b, flat), 1) & (rows - 1)))
-    found = dot(digits, spread)
-    place_of = found[:blocks] * 16.0 + found[blocks:] + 1.0
-    peer_row = (iota((1, flat), 1) >> log2(rows)) ^ me
-    seg_id = iota((seg_local, flat), 0).astype(F32)
-    for plane in range(2):
-        wanted = (peer_row * 2 + lax.rem(y + plane, 2)).astype(F32)
-        place = jnp.sum(jnp.where(key == wanted, place_of, 0.0), axis=0, keepdims=True) - 1.0
-        wt[plane] = one_hot(seg_id == place)
 
     for load in loads[1:]:
         load.wait()
@@ -174,9 +166,11 @@
     turn = one_hot(chosen)
     lperm[...] = dot(dot(turn, left_v[...]).astype(BF16), turn, ((1,), (1,))).astype(BF16)
 
-    for k in order[shards // 2:] + [0]:
+    for k in order[-1:] + [0]:
         pass_on(k)
     late = order[:-2] + [order[-1], order[-2]]
+    early = [order[2], order[0]] + sorted(set(range(1, shards // 2)) - {order[2]}, reverse=True) + order[1:2]
+    early += sorted(set(range(shards // 2, shards)) - set(order[:2]))
     waiting = list(late)
 
     def middle(n):
@@ -211,7 +205,16 @@
         z_back[k].start()
     ud[0, 0] = u[0]
     y_back[0].start()
-    for k in late:
+    spread = one_hot((iota((order_b, flat), 0) >> log2(shards)) == (iota((order_b, flat), 1) & (rows - 1)))
+    found = dot(digits, spread)
+    place_of = found[:blocks] * 16.0 + found[blocks:] + 1.0
+    peer_row = (iota((1, flat), 1) >> log2(rows)) ^ me
+    seg_id = iota((seg_local, flat), 0).astype(F32)
+    for plane in range(2):
+        wanted = (peer_row * 2 + lax.rem(y + plane, 2)).astype(F32)
+        place = jnp.sum(jnp.where(key == wanted, place_of, 0.0), axis=0, keepdims=True) - 1.0
+        wt[plane] = one_hot(seg_id == place)
+    for k in early:
         z_back[k].wait_recv()
         y_back[k].start()
 
@@ -220,7 +223,7 @@
         span = (high - low) * rows
         return sum(dot(wt[n, at, lanes], ud[n, low:high].reshape(span, half)) for n in range(2))
 
-    waiting = [0] + late
+    waiting = [0] + early
     low, high = spans[0]
     while any(low <= k < high for k in waiting):
         y_back[waiting.pop(0)].wait_recv()
@@ -245,20 +248,25 @@
         write.wait()
 
 
-def join(own_hbm, other_hbm, out_hbm, sem):
+def join(own_hbm, other_hbm, out_hbm, whole, in_sem, out_sem):
     c = lax.rem(lax.axis_index("rep"), 2)
     seg_local, half = own_hbm.shape
     step = seg_local // JOINS
-    copies = []
-    for n, (ref, side) in enumerate(((own_hbm, c), (other_hbm, 1 - c))):
-        lanes = pl.ds(pl.multiple_of(side * half, half), half)
-        for i in range(JOINS):
-            at = pl.ds(i * step, step)
-            copies.append(pltpu.make_async_copy(ref.at[at], out_hbm.at[at, lanes], sem.at[n, i]))
-    for copy in copies:
-        copy.start()
-    for copy in copies:
-        copy.wait()
+    reads, writes = [], []
+    for i in range(JOINS):
+        at = pl.ds(i * step, step)
+        for n, (ref, side) in enumerate(((own_hbm, c), (other_hbm, 1 - c))):
+            lanes = pl.ds(pl.multiple_of(side * half, half), half)
+            reads.append(pltpu.make_async_copy(ref.at[at], whole.at[at, lanes], in_sem.at[n, i]))
+            reads[-1].start()
+    for i in range(JOINS):
+        at = pl.ds(i * step, step)
+        reads[2 * i].wait()
+        reads[2 * i + 1].wait()
+        writes.append(pltpu.make_async_copy(whole.at[at], out_hbm.at[at], out_sem.at[i]))
+        writes[-1].start()
+    for write in writes:
+        write.wait()
 
 
 def on_device(grad_part, seg_slot, owner, left_code, left_scale, right_code, right_scale):
@@ -312,7 +320,11 @@
         out_shape=jax.ShapeDtypeStruct((seg_local, width), BF16),
         in_specs=[hbm, hbm],
         out_specs=hbm,
-        scratch_shapes=[pltpu.SemaphoreType.DMA((2, JOINS))],
+        scratch_shapes=[
+            pltpu.VMEM((seg_local, width), BF16),
+            pltpu.SemaphoreType.DMA((2, JOINS)),
+            pltpu.SemaphoreType.DMA((JOINS,)),
+        ],
         compiler_params=pltpu.CompilerParams(vmem_limit_bytes=60 * 1024 * 1024),
     )(own, other)
 

time: 52 us -> 36.1 us (0.69)
  Pallas kernels: 51.8 us -> 35.9 us
    pallas_call x1, Pallas kernels: 17.1 us -> 1.83 us  [on_device(): pl.pallas_call(join, out_shape=jax.ShapeDtypeStruct((seg_local, width), B...]
    pallas_call x1, Pallas kernels: 34.7 us -> 34.1 us  [on_device(): pl.pallas_call(functools.partial(kernel, shards), out_shape=[jax.ShapeDty...]
where the time goes in v5:
time: 36.1 us; the launch traced here: 35.9 us
  Pallas kernels  35.9 us (99%)
    pallas_call x1, Pallas kernels, on_device(): pl.pallas_call(functools.partial(kernel, shards), out_shape=[jax.ShapeDty...  34.1 us
    pallas_call x1, Pallas kernels, on_device(): pl.pallas_call(join, out_shape=jax.ShapeDtypeStruct((seg_local, width), B...  1.83 us

profile of v5, /device:TPU:0, one launch (start us, length us, event | category | flops | bytes accessed | tf_op | source)
XLA Modules:
  0.0 35.9 jit_solution(10482221661986829881)
XLA Ops:
  0.0 34.1 %shard_map.73 = (bf16[512,256]{1,0:T(8,128)(2,1)}, bf16[512,256]{1,0:T(8,128)(2,1)}) custom-call(s32[8,512]{1,0:T(8,128)} %seg_hbm.1, s32[1,8]{1,0:T(1,128)} %bitcast.1, f32[2,512]{1,0:T(2,128)} %lscale_hbm.1, f32[2,512]{1,0:T(2,128)} %rscale_hbm.1, bf16[1,512,512]{2,1,0:T(8,128)(2,1)} %grad_hbm.1, bf16[2,512,512]{2,1,0:T(8,128)(2,1)} %left_hbm.1, ...), custom_call_target="tpu_custom_call" | custom-call | tf_op jit(solution)/shard_map/pallas_call | solution.py:285
  34.1 1.8 %shard_map.74 = bf16[512,512]{1,0:T(8,128)(2,1)} custom-call(bf16[512,256]{1,0:T(8,128)(2,1)} %get-tuple-element.7.own_hbm, bf16[512,256]{1,0:T(8,128)(2,1)} %get-tuple-element.8.other_hbm), custom_call_target="tpu_custom_call" | custom-call | tf_op jit(solution)/shard_map/pallas_call | solution.py:318

commit v6 on v5

--- a/solution.py
+++ b/solution.py
@@ -41,11 +41,10 @@
 
 
 def send_order(shards):
-    far = list(range(shards // 2, shards))
-    near = [*range(shards // 4, shards // 2), *range(shards // 4 - 1, 0, -1)]
-    order = far[:2]
-    for n, k in enumerate(near):
-        order += [k] + far[n + 2:n + 3]
+    mid = shards // 2
+    order = []
+    for n in range(1, mid):
+        order += [mid + n, mid - n]
     return order
 
 
@@ -61,8 +60,15 @@
     rows = order_b // shards
     seg_local, half = p_own.shape
     flat = shards * rows
+    mid_label = shards // 2
+    flipped = partner(me, mid_label, shards)
+    origin = me + c * (flipped - me)
+    own, mate = c * mid_label, (1 - c) * mid_label
     order = send_order(shards)
-    peers = {k: partner(me, k, shards) for k in order}
+    peers = {k: partner(origin, k, shards) for k in order}
+    order = ["mate"] + order
+    label = {"mate": mate, "own": own, **{k: k for k in peers}}
+    peers["mate"] = flipped
     here = pl.ds(pl.multiple_of(c * half, half), half)
     there = pl.ds(pl.multiple_of((1 - c) * half, half), half)
 
@@ -82,6 +88,7 @@
     loads.append(pltpu.make_async_copy(rscale_hbm, rscale_ref, local_sem.at[9]))
 
     def send(kind, k, src, dst, rep_to, shard_to):
+        k = label.get(k, k)
         return pltpu.make_async_remote_copy(
             src_ref=src, dst_ref=dst, send_sem=send_sem.at[kind, k], recv_sem=recv_sem.at[kind, k],
             device_id={"rep": rep_to, "shard": shard_to}, device_id_type=MESH)
@@ -115,7 +122,7 @@
     same = own_col == own_row
     key_row = own_row * 2.0 + jnp.sum(jnp.where(same & (line_b < lane_b), 1.0, 0.0), axis=0, keepdims=True)
     key = own_col * 2.0 + jnp.sum(jnp.where(same & (lane_b < line_b), 1.0, 0.0), axis=1, keepdims=True)
-    peer_col = (iota((flat, 1), 0) >> log2(rows)) ^ me
+    peer_col = (iota((flat, 1), 0) >> log2(rows)) ^ origin
     seg_lane = iota((flat, seg_local), 1).astype(F32)
 
     def picked(plane):
@@ -128,25 +135,27 @@
     pair.wait_recv()
     q = (p_own[...].astype(F32) + p_got[...].astype(F32)).astype(BF16)
     f[1] = dot(pick_far, q).astype(BF16).reshape(shards, rows, half)
-    y_out = {k: send(Y_OUT, k, f.at[1, k], y_got.at[k], y_rep, me) for k in order + [0]}
-    for k in order + [0]:
+    y_out = {k: send(Y_OUT, k, f.at[1, label[k]], y_got.at[label[k]], y_rep, me) for k in order + ["own"]}
+    for k in order + ["own"]:
         y_out[k].start()
     f[0] = dot(picked(0), q).astype(BF16).reshape(shards, rows, half)
-    z_out = {k: send(Z_OUT, k, g.at[k], a.at[0, k], rep, peers[k]) for k in order}
+    z_out = {k: send(Z_OUT, k, g.at[label[k]], a.at[0, label[k]], rep, peers[k]) for k in order}
     quarter = shards // 4
-    spans = ((quarter, 3 * quarter), (0, quarter), (3 * quarter, shards))
-    c_out = {
-        n: send(C_OUT, n, a.at[0, low:high], a.at[1, low:high], c_rep, me) for n, (low, high) in enumerate(spans)
-    }
+    spans = ((2 * quarter, 3 * quarter), (quarter, 2 * quarter), (3 * quarter, shards), (0, quarter))
+    c_out = {}
+    for n, (low, high) in enumerate(spans):
+        to = (low + mid_label) % shards
+        c_out[n] = send(C_OUT, n, a.at[0, low:high], a.at[1, to:to + quarter], c_rep, me)
 
     def pass_on(k):
         y_out[k].wait_recv()
-        total = (f[0, k].astype(F32) + y_got[k].astype(F32)).astype(BF16)
-        if k:
-            g[k] = total
+        at = label[k]
+        total = (f[0, at].astype(F32) + y_got[at].astype(F32)).astype(BF16)
+        if k != "own":
+            g[at] = total
             z_out[k].start()
         else:
-            a[0, 0] = total
+            a[0, own] = total
 
     for k in order[:-1]:
         pass_on(k)
@@ -157,7 +166,7 @@
     first = (seg[:, 0:1] >> log2(seg_local)).astype(F32)
     shift = jnp.sum(jnp.where(mine, first, 0.0), axis=0, keepdims=True).astype(jnp.int32)
     line = iota((flat, 1), 0)
-    target = (line & (rows - 1)) * shards + ((((line >> log2(rows)) ^ me) - shift) & (shards - 1))
+    target = (line & (rows - 1)) * shards + ((((line >> log2(rows)) ^ origin) - shift) & (shards - 1))
     chosen = iota((flat, order_b), 1) == target
     lscale = jnp.where(y == 0, lscale_ref[0:1, :], lscale_ref[1:2, :])
     lscale = jnp.sum(jnp.where(chosen, lscale, 0.0), axis=1, keepdims=True)
@@ -166,16 +175,12 @@
     turn = one_hot(chosen)
     lperm[...] = dot(dot(turn, left_v[...]).astype(BF16), turn, ((1,), (1,))).astype(BF16)
 
-    for k in order[-1:] + [0]:
+    for k in order[-1:] + ["own"]:
         pass_on(k)
-    late = order[:-2] + [order[-1], order[-2]]
-    early = [order[2], order[0]] + sorted(set(range(1, shards // 2)) - {order[2]}, reverse=True) + order[1:2]
-    early += sorted(set(range(shards // 2, shards)) - set(order[:2]))
-    waiting = list(late)
+    waiting = list(order)
 
     def middle(n):
         low, high = spans[n]
-        c_out[n].wait_recv()
         span = (high - low) * rows
         mine_half = a[0, low:high].reshape(span, half)
         other_half = a[1, low:high].reshape(span, half)
@@ -184,14 +189,28 @@
         wide, wide_other = mine_half.astype(F32), other_half.astype(F32)
         return jnp.sum(wide * wide + wide_other * wide_other, keepdims=True)
 
+    landed = [(n, next(m for m, (low, _) in enumerate(spans) if low == (spans[n][0] + mid_label) % shards))
+              for n in range(len(spans))]
     grad_power = jnp.zeros((1, 1), F32)
+    started = set()
+    received = set()
     for n, (low, high) in enumerate(spans):
-        while any(low <= k < high for k in waiting):
+        while any(low <= k < high for k in waiting if k != "mate") or "mate" in waiting:
             z_out[waiting.pop(0)].wait_recv()
         c_out[n].start()
+        started.add(n)
         if n:
-            grad_power += middle(n - 1)
-    grad_power += middle(len(spans) - 1)
+            c_out[n - 1].wait_recv()
+            received.add(n - 1)
+        for here_n, from_n in landed:
+            if here_n in started and from_n in received:
+                grad_power += middle(here_n)
+                started.remove(here_n)
+    c_out[len(spans) - 1].wait_recv()
+    received.add(len(spans) - 1)
+    for here_n, from_n in landed:
+        if here_n in started:
+            grad_power += middle(here_n)
 
     precond = dot(lperm[...], mid[...]) * lscale
     update_power = jnp.sum(precond * precond, keepdims=True)
@@ -199,22 +218,22 @@
     ratio = jnp.sqrt((grad_power * scale + EPSILON) / (update_power * scale + EPSILON))
     u[...] = (precond[:, :half] * ratio).astype(BF16).reshape(shards, rows, half)
 
-    z_back = {k: send(Z_BACK, k, u.at[k], ud.at[0, k], rep, peers[k]) for k in order}
-    y_back = {k: send(Y_BACK, k, ud.at[0, k], ud.at[1, k], y_rep, me) for k in order + [0]}
+    z_back = {k: send(Z_BACK, k, u.at[label[k]], ud.at[0, label[k]], rep, peers[k]) for k in order}
+    y_back = {k: send(Y_BACK, k, ud.at[0, label[k]], ud.at[1, label[k]], y_rep, me) for k in order + ["own"]}
     for k in order:
         z_back[k].start()
-    ud[0, 0] = u[0]
-    y_back[0].start()
+    ud[0, own] = u[own]
+    y_back["own"].start()
     spread = one_hot((iota((order_b, flat), 0) >> log2(shards)) == (iota((order_b, flat), 1) & (rows - 1)))
     found = dot(digits, spread)
     place_of = found[:blocks] * 16.0 + found[blocks:] + 1.0
-    peer_row = (iota((1, flat), 1) >> log2(rows)) ^ me
+    peer_row = (iota((1, flat), 1) >> log2(rows)) ^ origin
     seg_id = iota((seg_local, flat), 0).astype(F32)
     for plane in range(2):
         wanted = (peer_row * 2 + lax.rem(y + plane, 2)).astype(F32)
         place = jnp.sum(jnp.where(key == wanted, place_of, 0.0), axis=0, keepdims=True) - 1.0
         wt[plane] = one_hot(seg_id == place)
-    for k in early:
+    for k in order:
         z_back[k].wait_recv()
         y_back[k].start()
 
@@ -223,17 +242,16 @@
         span = (high - low) * rows
         return sum(dot(wt[n, at, lanes], ud[n, low:high].reshape(span, half)) for n in range(2))
 
-    waiting = [0] + early
-    low, high = spans[0]
-    while any(low <= k < high for k in waiting):
+    waiting = ["own"] + order
+    while any(k in waiting for k in ["mate"] + [k for k in order[1:] if quarter <= k < 3 * quarter]):
         y_back[waiting.pop(0)].wait_recv()
-    acc[...] = placed(slice(None), low, high)
+    acc[...] = placed(slice(None), quarter, 3 * quarter)
     for k in waiting:
         y_back[k].wait_recv()
     c_back, writes = {}, []
     for n in range(2):
         at = slice(n * seg_local // 2, (n + 1) * seg_local // 2)
-        done[at] = (acc[at] + placed(at, *spans[1]) + placed(at, *spans[2])).astype(BF16)
+        done[at] = (acc[at] + placed(at, 0, quarter) + placed(at, 3 * quarter, shards)).astype(BF16)
         c_back[n] = send(C_BACK, n, done.at[at], other_hbm.at[at], c_rep, me)
         c_back[n].start()
         writes.append(pltpu.make_async_copy(done.at[at], own_hbm.at[at], local_sem.at[n]))

time: 36.1 us -> 36.5 us (1.011)
  Pallas kernels: 35.9 us -> 36.3 us
    pallas_call x1, Pallas kernels: 34.1 us -> 34.5 us  [on_device(): pl.pallas_call(functools.partial(kernel, shards), out_shape=[jax.ShapeDty...]
where the time goes in v6:
time: 36.5 us; the launch traced here: 36.3 us
  Pallas kernels  36.3 us (99%)
    pallas_call x1, Pallas kernels, on_device(): pl.pallas_call(functools.partial(kernel, shards), out_shape=[jax.ShapeDty...  34.5 us
    pallas_call x1, Pallas kernels, on_device(): pl.pallas_call(join, out_shape=jax.ShapeDtypeStruct((seg_local, width), B...  1.83 us

profile of v6, /device:TPU:0, one launch (start us, length us, event | category | flops | bytes accessed | tf_op | source)
XLA Modules:
  0.0 36.3 jit_solution(63699855410122170)
XLA Ops:
  0.0 34.5 %shard_map.73 = (bf16[512,256]{1,0:T(8,128)(2,1)}, bf16[512,256]{1,0:T(8,128)(2,1)}) custom-call(s32[8,512]{1,0:T(8,128)} %seg_hbm.1, s32[1,8]{1,0:T(1,128)} %bitcast.1, f32[2,512]{1,0:T(2,128)} %lscale_hbm.1, f32[2,512]{1,0:T(2,128)} %rscale_hbm.1, bf16[1,512,512]{2,1,0:T(8,128)(2,1)} %grad_hbm.1, bf16[2,512,512]{2,1,0:T(8,128)(2,1)} %left_hbm.1, ...), custom_call_target="tpu_custom_call" | custom-call | tf_op jit(solution)/shard_map/pallas_call | solution.py:303
  34.5 1.8 %shard_map.74 = bf16[512,512]{1,0:T(8,128)(2,1)} custom-call(bf16[512,256]{1,0:T(8,128)(2,1)} %get-tuple-element.7.own_hbm, bf16[512,256]{1,0:T(8,128)(2,1)} %get-tuple-element.8.other_hbm), custom_call_target="tpu_custom_call" | custom-call | tf_op jit(solution)/shard_map/pallas_call | solution.py:336

commit v7 on v5

--- a/solution.py
+++ b/solution.py
@@ -12,7 +12,7 @@
 F32 = jnp.float32
 BF16 = jnp.bfloat16
 Y_OUT, Z_OUT, C_OUT, Z_BACK, Y_BACK, C_BACK, PAIR = range(7)
-JOINS = 4
+JOINS = 2
 
 
 def log2(value):
@@ -52,7 +52,7 @@
 def kernel(
     shards, seg_hbm, owner_hbm, lscale_hbm, rscale_hbm, grad_hbm, left_hbm, right_hbm,
     own_hbm, other_hbm,
-    seg_ref, owner_ref, lscale_ref, rscale_ref, p_own, p_got, wt, f, y_got, g, a, left_v, right_v, lperm, mid, u, ud, acc, done, local_sem, send_sem, recv_sem,
+    seg_ref, owner_ref, lscale_ref, rscale_ref, p_own, p_got, wt, f, y_got, g, a, left_v, right_v, lperm, mid, partial, u, ud, acc, done, local_sem, send_sem, recv_sem,
 ):
     rep, me = lax.axis_index("rep"), lax.axis_index("shard")
     y, c = lax.rem(lax.div(rep, 2), 2), lax.rem(rep, 2)
@@ -127,14 +127,19 @@
     loads[0].wait()
     pair.wait_recv()
     q = (p_own[...].astype(F32) + p_got[...].astype(F32)).astype(BF16)
-    f[1] = dot(pick_far, q).astype(BF16).reshape(shards, rows, half)
+    quarter = shards // 4
+    spans = ((quarter, 3 * quarter), (0, quarter), (3 * quarter, shards))
     y_out = {k: send(Y_OUT, k, f.at[1, k], y_got.at[k], y_rep, me) for k in order + [0]}
-    for k in order + [0]:
+    unsent = order + [0]
+    for n, (low, high) in enumerate(spans):
+        part = dot(pick_far[low * rows:high * rows], q)
+        f[1, low:high] = part.astype(BF16).reshape(high - low, rows, half)
+        while unsent and n == 0 and low <= unsent[0] < high:
+            y_out[unsent.pop(0)].start()
+    for k in unsent:
         y_out[k].start()
     f[0] = dot(picked(0), q).astype(BF16).reshape(shards, rows, half)
     z_out = {k: send(Z_OUT, k, g.at[k], a.at[0, k], rep, peers[k]) for k in order}
-    quarter = shards // 4
-    spans = ((quarter, 3 * quarter), (0, quarter), (3 * quarter, shards))
     c_out = {
         n: send(C_OUT, n, a.at[0, low:high], a.at[1, low:high], c_rep, me) for n, (low, high) in enumerate(spans)
     }
@@ -191,9 +196,11 @@
         c_out[n].start()
         if n:
             grad_power += middle(n - 1)
+    known = 3 * quarter * rows
+    partial[...] = dot(lperm[:, :known], mid[:known])
     grad_power += middle(len(spans) - 1)
 
-    precond = dot(lperm[...], mid[...]) * lscale
+    precond = (partial[...] + dot(lperm[:, known:], mid[known:])) * lscale
     update_power = jnp.sum(precond * precond, keepdims=True)
     scale = 1.0 / (order_b * 2 * half)
     ratio = jnp.sqrt((grad_power * scale + EPSILON) / (update_power * scale + EPSILON))
@@ -303,6 +310,7 @@
             pltpu.VMEM((2, half, width), BF16),
             pltpu.VMEM((flat, flat), BF16),
             pltpu.VMEM((flat, width), BF16),
+            pltpu.VMEM((flat, width), F32),
             pltpu.VMEM((shards, rows, half), BF16),
             pltpu.VMEM((2, shards, rows, half), BF16),
             pltpu.VMEM((seg_local, half), F32),

time: 36.1 us -> 35.9 us (level)
  no operation moved by 1% of the time
where the time goes in v7:
time: 35.9 us; the launch traced here: 35.8 us
  Pallas kernels  35.8 us (100%)
    pallas_call x1, Pallas kernels, on_device(): pl.pallas_call(functools.partial(kernel, shards), out_shape=[jax.ShapeDty...  33.9 us
    pallas_call x1, Pallas kernels, on_device(): pl.pallas_call(join, out_shape=jax.ShapeDtypeStruct((seg_local, width), B...  1.86 us

profile of v7, /device:TPU:0, one launch (start us, length us, event | category | flops | bytes accessed | tf_op | source)
XLA Modules:
  0.0 35.8 jit_solution(13369562460329625387)
XLA Ops:
  0.0 33.9 %shard_map.73 = (bf16[512,256]{1,0:T(8,128)(2,1)}, bf16[512,256]{1,0:T(8,128)(2,1)}) custom-call(s32[8,512]{1,0:T(8,128)} %seg_hbm.1, s32[1,8]{1,0:T(1,128)} %bitcast.1, f32[2,512]{1,0:T(2,128)} %lscale_hbm.1, f32[2,512]{1,0:T(2,128)} %rscale_hbm.1, bf16[1,512,512]{2,1,0:T(8,128)(2,1)} %grad_hbm.1, bf16[2,512,512]{2,1,0:T(8,128)(2,1)} %left_hbm.1, ...), custom_call_target="tpu_custom_call" | custom-call | tf_op jit(solution)/shard_map/pallas_call | solution.py:292
  33.9 1.9 %shard_map.74 = bf16[512,512]{1,0:T(8,128)(2,1)} custom-call(bf16[512,256]{1,0:T(8,128)(2,1)} %get-tuple-element.7.own_hbm, bf16[512,256]{1,0:T(8,128)(2,1)} %get-tuple-element.8.other_hbm), custom_call_target="tpu_custom_call" | custom-call | tf_op jit(solution)/shard_map/pallas_call | solution.py:326

commit v8 on v7

--- a/solution.py
+++ b/solution.py
@@ -212,6 +212,11 @@
         z_back[k].start()
     ud[0, 0] = u[0]
     y_back[0].start()
+    mid_way = shards // 2
+    for k in early[:mid_way]:
+        z_back[k].wait_recv()
+        y_back[k].start()
+
     spread = one_hot((iota((order_b, flat), 0) >> log2(shards)) == (iota((order_b, flat), 1) & (rows - 1)))
     found = dot(digits, spread)
     place_of = found[:blocks] * 16.0 + found[blocks:] + 1.0
@@ -221,7 +226,7 @@
         wanted = (peer_row * 2 + lax.rem(y + plane, 2)).astype(F32)
         place = jnp.sum(jnp.where(key == wanted, place_of, 0.0), axis=0, keepdims=True) - 1.0
         wt[plane] = one_hot(seg_id == place)
-    for k in early:
+    for k in early[mid_way:]:
         z_back[k].wait_recv()
         y_back[k].start()
 

time: 35.9 us -> 35.9 us (level)
  no operation moved by 1% of the time
where the time goes in v8:
time: 35.9 us; the launch traced here: 35.7 us
  Pallas kernels  35.7 us (99%)
    pallas_call x1, Pallas kernels, on_device(): pl.pallas_call(functools.partial(kernel, shards), out_shape=[jax.ShapeDty...  33.8 us
    pallas_call x1, Pallas kernels, on_device(): pl.pallas_call(join, out_shape=jax.ShapeDtypeStruct((seg_local, width), B...  1.86 us

profile of v8, /device:TPU:0, one launch (start us, length us, event | category | flops | bytes accessed | tf_op | source)
XLA Modules:
  0.0 35.7 jit_solution(1005094639612515251)
XLA Ops:
  0.0 33.8 %shard_map.73 = (bf16[512,256]{1,0:T(8,128)(2,1)}, bf16[512,256]{1,0:T(8,128)(2,1)}) custom-call(s32[8,512]{1,0:T(8,128)} %seg_hbm.1, s32[1,8]{1,0:T(1,128)} %bitcast.1, f32[2,512]{1,0:T(2,128)} %lscale_hbm.1, f32[2,512]{1,0:T(2,128)} %rscale_hbm.1, bf16[1,512,512]{2,1,0:T(8,128)(2,1)} %grad_hbm.1, bf16[2,512,512]{2,1,0:T(8,128)(2,1)} %left_hbm.1, ...), custom_call_target="tpu_custom_call" | custom-call | tf_op jit(solution)/shard_map/pallas_call | solution.py:297
  33.9 1.9 %shard_map.74 = bf16[512,512]{1,0:T(8,128)(2,1)} custom-call(bf16[512,256]{1,0:T(8,128)(2,1)} %get-tuple-element.7.own_hbm, bf16[512,256]{1,0:T(8,128)(2,1)} %get-tuple-element.8.other_hbm), custom_call_target="tpu_custom_call" | custom-call | tf_op jit(solution)/shard_map/pallas_call | solution.py:331
